TPU v7x, 128 devices: a whole 4x4x4 slice. The times are simulated.
128 devices in a mesh: dp: 4 (over x_hi, core), fsdp: 32 (over z, x_lo, y).
Axes of the slice: x: 4 (x_hi: 2, x_lo: 2; x = x_hi * 2 + x_lo), y: 4, z: 4, core: 2. Of those that a mesh axis runs over, the one named last changes fastest.
Arguments:
- tokens: bfloat16 [128, 128, 1024], P(('dp', 'fsdp')), may hold values from -6 to 6
- cotangent: bfloat16 [128, 128, 1024], P(('dp', 'fsdp')), may hold values from -6 to 6
- segment: int32 [128, 128], P(('dp', 'fsdp')), may hold values from 0 to 31, never falling along the last dimension, each value on 1 to 64 neighbouring positions
- keep_mask: int32 [128, 128], P(('dp', 'fsdp')), may hold values 0 or 1
- conv_state: float32 [128, 3, 1536], P(('dp', 'fsdp')), may hold values from -6 to 6
- lru_state: float32 [128, 1536], P(('dp', 'fsdp')), may hold values from -6 to 6
- norm1_gain: bfloat16 [1024], P(('dp', 'fsdp')), may hold values from 0.099609375 to 1.8984375
- conv_weight: bfloat16 [4, 1536], P(None, ('dp', 'fsdp')), may hold values from -3 to 3
- lru_bias: bfloat16 [3, 1536], P(None, ('dp', 'fsdp')), may hold values from -4 to 4
- decay_rate: bfloat16 [1536], P(('dp', 'fsdp')), may hold values from 0.00029945374 to 0.029907227
- gate_weight: bfloat16 [1536, 384], P(('dp', 'fsdp')), may hold values from -0.4375 to 0.4375
- branch_weight: bfloat16 [1024, 3072], P(('dp', 'fsdp')), may hold values from -0.1875 to 0.1875
- out_weight: bfloat16 [1536, 1024], P(('dp', 'fsdp')), may hold values from -0.625 to 0.625
- norm2_gain: bfloat16 [1024], P(('dp', 'fsdp')), may hold values from 0.099609375 to 1.8984375
- mlp_in_weight: bfloat16 [1024, 6144], P(('dp', 'fsdp')), may hold values from -0.1875 to 0.1875
- mlp_out_weight: bfloat16 [3072, 1024], P(('dp', 'fsdp')), may hold values from -0.15625 to 0.15625
Outputs:
- output: bfloat16 [128, 128, 1024], P(('dp', 'fsdp'))
- input_grad: bfloat16 [128, 128, 1024], P(('dp', 'fsdp'))
- final_conv: float32 [128, 3, 1536], P(('dp', 'fsdp'))
- final_state: float32 [128, 1536], P(('dp', 'fsdp'))
- norm1_gain_grad: float32 [1024], P(('dp', 'fsdp'))
- conv_weight_grad: float32 [4, 1536], P(None, ('dp', 'fsdp'))
- lru_bias_grad: float32 [3, 1536], P(None, ('dp', 'fsdp'))
- decay_rate_grad: float32 [1536], P(('dp', 'fsdp'))
- gate_weight_grad: float32 [1536, 384], P(('dp', 'fsdp'))
- branch_weight_grad: float32 [1024, 3072], P(('dp', 'fsdp'))
- out_weight_grad: float32 [1536, 1024], P(('dp', 'fsdp'))
- norm2_gain_grad: float32 [1024], P(('dp', 'fsdp'))
- mlp_in_weight_grad: float32 [1024, 6144], P(('dp', 'fsdp'))
- mlp_out_weight_grad: float32 [3072, 1024], P(('dp', 'fsdp'))
Inputs may be any that keep to these rules, and one draw needn't show every extreme that they name: `segment`: segment numbers never fall along a sequence; a position whose number differs from the one before starts a new document.
All inputs are finite; a program needn't handle non-finite values. No bound on the sum of `keep_mask` on one device may be relied on, other than what follows from the above.
Results may differ from a plain program's by a relative error of at most 0.013.
Values may be sent and summed in bfloat16 or wider, within the bound.
No kernel may reach another device: no remote copies, remote signals or barrier semaphores. Data moves between devices by JAX's collectives and lax.ppermute only.
A program may use at most 256 MiB of HBM per device.

v0:
```python
import jax
import jax.numpy as jnp
from jax import lax
from jax.experimental import pallas as pl
from jax.experimental.pallas import tpu as pltpu
from jax.sharding import PartitionSpec as P

AXES = ("dp", "fsdp")
D, R, F, SEQ = 1024, 1536, 3072, 128
RC, FC = R // 2, F // 2
HS = 192
F32, BF16 = jnp.float32, jnp.bfloat16
BRANCH, INNER = 2 * RC, 2 * FC
TOK, PAD, LANES = 2 * SEQ, SEQ + 8, 128

EARLY, LATE = 1408, 2304
UNIT = EARLY + LATE
OG, PB, PI, QB = 1152, 256, 768, 1280
DC = PB + PI + UNIT
OGC = 1536
DOWN = DC + OGC
OWN = DOWN + D + D // 2


def place_of(device):
    outer, inner = divmod(device, 32)
    x_hi, core = divmod(outer, 2)
    z, rest = divmod(inner, 8)
    x_lo, y = divmod(rest, 4)
    return dict(x=x_hi * 2 + x_lo, y=y, z=z, core=core)


def device_at(x, y, z, core):
    return ((x // 2) * 2 + core) * 32 + z * 8 + (x % 2) * 4 + y


def pairs(move):
    return [(d, device_at(**move(place_of(d)))) for d in range(128)]


def along(axis, steps):
    def move(p):
        sign = 1 if p["core"] == 0 else -1
        return {**p, axis: (p[axis] + sign * steps) % 4}

    return pairs(move)


def other_core(p):
    return {**p, "core": 1 - p["core"]}


def partner(axis, turn):
    def move(p):
        i = p[axis]
        return {**p, axis: i ^ 1 if (p["core"] + turn) % 2 == 0 else 3 - i}

    return pairs(move)


def opposite(axis):
    return pairs(lambda p: {**p, axis: (p[axis] + 2) % 4})


def send(value, route):
    return lax.ppermute(value, AXES, route)


def swap(value):
    return send(value, pairs(other_core))


def my_place():
    device = lax.axis_index(AXES)
    outer, inner = device // 32, device % 32
    return dict(x=(outer // 2) * 2 + (inner // 4) % 2, y=inner % 4, z=inner // 8, core=outer % 2)


def ring_places(axis, here):
    sign, at = 1 - 2 * here["core"], here[axis]
    return [at, (at - sign) % 4, (at + sign) % 4, (at + 2) % 4]


def ring(block, axis):
    one = send(block, along(axis, 1))
    two = send(one, along(axis, 1))
    return block, one, send(two, along(axis, 1)), two


def ring_both(block, axis):
    up, down = send(block, along(axis, 1)), send(block, along(axis, -1))
    return block, up, down, send(up, along(axis, 1))


def pair_places(axis, here):
    i, odd = here[axis], here["core"] == 1
    by_one, by_ends = i + 1 - 2 * (i % 2), 3 - i
    return [i, jnp.where(odd, by_one, by_ends), jnp.where(odd, by_ends, by_one), (i + 2) % 4]


def ring_direct(block, axis):
    return block, send(block, along(axis, 1)), send(block, along(axis, -1)), send(block, opposite(axis))


def terms_direct(terms, axis):
    own, ahead, far, behind = terms
    return own, send(ahead, along(axis, 1)), send(far, opposite(axis)), send(behind, along(axis, -1))


def total(*terms):
    out = terms[0].astype(F32)
    for term in terms[1:]:
        out = out + term.astype(F32)
    return out.astype(BF16)


def core_half(array, core, blocks):
    v = array.reshape(array.shape[:-1] + (blocks, 2, array.shape[-1] // (2 * blocks)))
    v = lax.dynamic_index_in_dim(v, core, v.ndim - 2, keepdims=False)
    return v.reshape(array.shape[:-1] + (array.shape[-1] // 2,))


def dot(a, b, dims):
    return lax.dot_general(a, b, (dims, ((), ())), preferred_element_type=F32)


def nn(a, b):
    return dot(a, b, ((1,), (0,)))


def nt(a, b):
    return dot(a, b, ((1,), (1,)))


def tn(a, b):
    return dot(a, b, ((0,), (0,)))


def inv_rms(v):
    return lax.rsqrt(jnp.mean(v * v, axis=-1, keepdims=True) + 1e-6)


def rms_back(grad, v, gain):
    s = inv_rms(v)
    n = v * s
    g2 = grad * gain
    return s * (g2 - n * jnp.mean(g2 * n, axis=-1, keepdims=True)), grad * n


C0, C1 = 0.7978845608028654, 0.044715


def gelu_both(a):
    t = jnp.tanh(C0 * (a + C1 * (a * a * a)))
    half = 0.5 * (1.0 + t)
    return a * half, half + 0.5 * a * (1.0 - t * t) * (C0 * (1.0 + 3.0 * C1 * (a * a)))


def gates(rate, inp, bias1, bias2, decay, keep, starts):
    rg = jax.nn.sigmoid(rate + bias1)
    ig = jax.nn.sigmoid(inp + bias2)
    sd = jnp.exp(-8.0 * rg * decay)
    q = 1.0 - sd * sd
    root = jnp.sqrt(jnp.maximum(q, 0.001))
    scale = starts + (1.0 - starts) * root
    return rg, ig, sd, q, root, scale


def cols(c):
    return pl.ds(pl.multiple_of(c * LANES, LANES), LANES)


class Saves:
    def __init__(self, sem):
        self.sem, self.copies = sem, []

    def start(self, source, target):
        self.copies.append(pltpu.make_async_copy(source, target, self.sem.at[len(self.copies)]))
        self.copies[-1].start()

    def wait(self):
        for copy in self.copies:
            copy.wait()


def pick(rows, where):
    return jnp.where(lax.broadcasted_iota(jnp.int32, (rows, where.shape[1]), 0) == where, 1.0, 0.0).astype(BF16)


def stand(values, rows):
    v = values.astype(F32)
    i = lax.broadcasted_iota(jnp.int32, (rows, v.shape[1]), 0)
    j = lax.broadcasted_iota(jnp.int32, (rows, v.shape[1]), 1)
    lane = lax.broadcasted_iota(jnp.int32, (rows, LANES), 1)
    out = jnp.zeros((rows, LANES), F32)
    for n in range(v.shape[0]):
        column = jnp.sum(jnp.where(i == j, v[n : n + 1], 0.0), axis=1, keepdims=True)
        out = out + jnp.where(lane == n, column, 0.0)
    return out


def load(sources, targets, sems):
    copies = Saves(sems)
    for source, target in zip(sources, targets):
        copies.start(source, target)
    copies.wait()


def pack(
    places, i_branch, i_inner, gain, i_out, i_gate, perchan, i_down, mine, theirs, own,
    branch, inner, out, gate, down, sems,
):
    load((i_branch, i_inner, i_out, i_gate, i_down), (branch, inner, out, gate, down), sems)

    gains = stand(gain[...], 8).astype(BF16)

    def halves(outs):
        for c, to_core in enumerate(outs):
            for q in range(4):
                v = branch[:, 768 * q + 384 * c : 768 * q + 384 * c + 384]
                if q == 0:
                    to_core[:, 0:PB] = v[:, 0:PB]
                    to_core[:, PB + PI : PB + PI + 128] = v[:, PB:]
                else:
                    to_core[:, PI + 384 * q : PI + 384 * q + 384] = v
                v = inner[:, 1536 * q + 768 * c : 1536 * q + 768 * c + 768]
                to = PB if q == 0 else DC - LATE + 768 * (q - 1)
                to_core[:, to : to + 768] = v
            tile = DC - LATE - LANES
            to_core[:, tile : tile + LANES] = gains

    @pl.when(places[3, 0] == 0)
    def _():
        halves((mine, theirs))

    @pl.when(places[3, 0] == 1)
    def _():
        halves((theirs, mine))

    own[...] = jnp.zeros_like(own)
    own[0:12, 0:D] = out[...]
    own[0:12, D : D + 384] = gate[...]
    own[:, 1408:OGC] = stand(perchan[...], 16).astype(BF16)
    own[:, OGC : OGC + D] = down[0:16]
    own[:, OGC + D :] = jnp.concatenate(
        [down[16:24, 0:512].astype(F32), down[16:24, 512:].astype(F32)], axis=0
    ).astype(BF16)


def join(places, mine, theirs, own, block):
    def rows(low, high):
        block[:, 0:DC] = jnp.concatenate([low[...].astype(F32), high[...].astype(F32)], axis=0).astype(BF16)

    @pl.when(places[3, 0] == 0)
    def _():
        rows(mine, theirs)

    @pl.when(places[3, 0] == 1)
    def _():
        rows(theirs, mine)

    block[:, DC:] = own[...]


def unit(places, p0, p1, p2, p3, *rest):
    o_p, o_q, p, q, d, dn, sems = rest[-7:]
    ogs = []
    s = lax.broadcasted_iota(jnp.int32, (1, 64), 1)
    y = jnp.zeros((1, 64), jnp.int32)
    for j, piece in enumerate((p0, p1, p2, p3)):
        at = places[1, j]
        y = jnp.where(s // 16 == j, at, y)
        v = piece[:, 0:DC].astype(F32)
        for c in range(2):
            d[pl.ds(pl.multiple_of(c * 32 + at * 8, 8), 8)] = v[8 * c : 8 * c + 8]
        ogs.append(piece[:, DC:DOWN])
        v = piece[:, DOWN:].astype(F32)
        dn[pl.ds(pl.multiple_of(at * 24, 8), 16)] = v[:, 0:D]
        for h in range(2):
            dn[pl.ds(pl.multiple_of(at * 24 + 16, 8), 8), 512 * h : 512 * h + 512] = v[8 * h : 8 * h + 8, D:]
    saves = Saves(sems)
    q[...] = d[:, PB + PI :].astype(BF16)
    for c in range(2):
        saves.start(q.at[pl.ds(32 * c, 32)], o_q.at[c])
    p[:, OG:EARLY] = d[:, 0:PB].astype(BF16)
    p[:, UNIT - PI :] = d[:, PB : PB + PI].astype(BF16)
    i = s % 16
    og = nn(pick(48, jnp.where(i < 12, y * 12 + i, 64)), jnp.concatenate(ogs, axis=0)).astype(BF16)
    p[0:48, 0:OG] = og[:, 0:OG]
    for r in range(3):
        p[48:64, 384 * r : 384 * r + 384] = og[16 * r : 16 * r + 16, OG:]
    p[:, EARLY : EARLY + D] = dn[0:64].astype(BF16)
    p[0:32, EARLY + D : EARLY + FC] = dn[64:96, 0:512].astype(BF16)
    p[32:64, EARLY + D : EARLY + FC] = dn[64:96, 512:1024].astype(BF16)
    for c in range(2):
        saves.start(p.at[pl.ds(32 * c, 32)], o_p.at[c])
    saves.wait()


def planes(which):
    def body(places, *refs):
        n = len(which)
        (o_pe, o_qe, o_pl, o_ql), v, in_sems, out_sems = refs[-7:-3], *refs[-3:]
        loads, saves = Saves(in_sems), Saves(out_sems)
        for i, piece in enumerate(refs[: 2 * n]):
            loads.start(piece, v.at[i])
        for i in range(2 * n):
            loads.copies[i].wait()
            j = which[i % n]
            x = places[0, j]
            for first, count, p, q in ((0, EARLY, o_pe, o_qe), (EARLY, LATE, o_pl, o_ql)):
                target = p.at[:, places[2, j]] if i < n else q.at[x // 2, :, x % 2]
                saves.start(v.at[i, :, :, pl.ds(first, count)], target)
        saves.wait()

    return body


ROWS = (2, 2, 4, 2, 32)
OG_ROWS, DOWN_ROWS = (2, 4, 2, 48), (2, 4, 2, 96)


def ring_rows(x, z):
    return (x // 2) * 512 + z * 64 + (x % 2) * 32


def p_copy(piece, places, j, first, count, block, to, sem):
    x = places[0, j]
    target = block.at[x // 2, :, :, x % 2, :, pl.ds(to, count)]
    pltpu.make_async_copy(piece.at[..., pl.ds(first, count)], target, sem).start()


def q_copy(piece, places, j, first, count, block, to, sem):
    target = block.at[:, :, places[2, j], :, :, pl.ds(to, count)]
    pltpu.make_async_copy(piece.at[..., pl.ds(first, count)], target, sem).start()


def og_copy(piece, places, j, block, sem):
    x = places[0, j]
    block = block.at[x // 2, :, x % 2]
    for source, target in (
        (piece.at[0, :, :, pl.ds(0, OG)], block.at[:, pl.ds(0, 32), pl.ds(0, OG)]),
        (piece.at[1, :, pl.ds(0, 16), pl.ds(0, OG)], block.at[:, pl.ds(32, 16), pl.ds(0, OG)]),
    ):
        pltpu.make_async_copy(source, target, sem).start()
    for r in range(3):
        pltpu.make_async_copy(
            piece.at[1, :, pl.ds(16, 16), pl.ds(384 * r, 384)], block.at[:, pl.ds(16 * r, 16), pl.ds(OG, 384)], sem
        ).start()


def down_copy(piece, places, j, block, sem):
    x = places[0, j]
    block = block.at[x // 2, :, x % 2]
    for h in range(2):
        pltpu.make_async_copy(piece.at[h, :, :, pl.ds(0, D)], block.at[:, pl.ds(32 * h, 32)], sem).start()
        pltpu.make_async_copy(
            piece.at[h, :, :, pl.ds(D, 512)], block.at[:, pl.ds(64, 32), pl.ds(512 * h, 512)], sem
        ).start()


def rows_of(block, first, count):
    return block[..., first : first + count].reshape(D, count)


def landed(block, sem):
    pltpu.make_async_copy(block, block, sem).wait()


def turn_matrix():
    i = lax.broadcasted_iota(jnp.int32, (2 * HS, 2 * HS), 0)
    j = lax.broadcasted_iota(jnp.int32, (2 * HS, 2 * HS), 1)
    return jnp.where((i == j + HS) | (j == i + HS), 1.0, 0.0).astype(BF16)


def quarter_masks():
    i = lax.broadcasted_iota(jnp.int32, (2 * HS, 2 * HS), 0) < HS
    j = lax.broadcasted_iota(jnp.int32, (2 * HS, 2 * HS), 1) < HS
    return i, j


def rec_forward(
    places, tok, masks, conv_before, lru_before, p0, p1, p2, p3, q0, q1, q2, q3,
    part, finals, gains, chans, o_normed, o_merged, o_u, o_gate, o_conv, o_rate, o_inp, o_st, o_tables,
    wb, wog, normed, merged, u, gate_in, conv_low, rate, inp, st, tables, coeff, drive, sems, out_sems,
):
    for j, (p, q) in enumerate(((p0, q0), (p1, q1), (p2, q2), (p3, q3))):
        p_copy(p, places, j, OG, PB, wb, 0, sems.at[0])
        q_copy(q, places, j, 0, EARLY, wb, PB, sems.at[0])
    for j, p in enumerate((p0, p1, p2, p3)):
        og_copy(p, places, j, wog, sems.at[1])
    saves = Saves(out_sems)
    t = tok[...].astype(F32)
    scaled = t * inv_rms(t)
    landed(wb, sems.at[0])
    gains[...] = rows_of(wb, BRANCH, LANES).astype(F32).T[:8]
    normed[...] = (scaled * gains[0:1]).astype(BF16)
    saves.start(normed, o_normed)
    for s in range(2):
        u[s, 0:8] = jnp.zeros((8, RC), F32)
        u[s, 5:8] = conv_before[s]
        st[s, 0:8] = jnp.zeros((8, RC), F32)
        st[s, 7:8] = lru_before[s]

    v = nn(normed[...], rows_of(wb, 0, RC))
    for s in range(2):
        rows = slice(s * SEQ, (s + 1) * SEQ)
        for c in range(6):
            u[s, 8:, LANES * c : LANES * c + LANES] = v[rows, LANES * c : LANES * c + LANES] * masks[0, rows]

    saves.start(u, o_u)

    gate_in[...] = nn(normed[...], rows_of(wb, RC, RC))

    saves.start(gate_in, o_gate)
    landed(wog, sems.at[1])
    chans[...] = wog[..., 1408:].reshape(RC, LANES).astype(F32).T[:8]

    @pl.loop(0, 6)
    def _(c):
        at = cols(c)
        for s in range(2):
            rows = slice(s * SEQ, (s + 1) * SEQ)
            v = chans[4:5, at] + chans[0:1, at] * u[s, 8:, at]
            for k in range(1, 4):
                v = v + chans[k : k + 1, at] * (u[s, 8 - k : PAD - k, at] * masks[1 + k, rows])
            conv_low[rows, at] = v.astype(BF16)

    saves.start(conv_low, o_conv)
    turn = turn_matrix()
    top, left = quarter_masks()
    for p in range(2):
        g = wog[p, :, :, :, D : D + 384].reshape(2 * HS, 2 * HS)
        turned = nn(g, turn).astype(BF16)
        zero = jnp.zeros_like(g)
        tables[2 * p] = jnp.where(left, jnp.where(top, g, zero), jnp.where(top, zero, turned))
        tables[2 * p + 1] = jnp.where(left, jnp.where(top, turned, zero), jnp.where(top, zero, g))
        at = slice(2 * HS * p, 2 * HS * (p + 1))
        rate[:, at] = nn(conv_low[:, at], tables[2 * p])
        inp[:, at] = nn(conv_low[:, at], tables[2 * p + 1])
    saves.start(tables, o_tables)
    saves.start(rate, o_rate)
    saves.start(inp, o_inp)

    @pl.loop(0, 6)
    def _(c):
        at = cols(c)
        keep, starts = masks[0], masks[1]
        _, ig, sd, _, _, scale = gates(
            rate[:, at], inp[:, at], chans[5:6, at], chans[6:7, at], chans[7:8, at], keep, starts
        )
        coeff[:, at] = (1.0 - starts) * (keep * sd + (1.0 - keep))
        drive[:, at] = keep * scale * ig * conv_low[:, at].astype(F32)

    row = lax.broadcasted_iota(jnp.int32, (8, RC), 0)

    def forward(i, carry):
        new = []
        for s in range(2):
            at = pl.ds(pl.multiple_of(s * SEQ + i * 8, 8), 8)
            a, b = coeff[at], drive[at]
            for k in (1, 2, 4):
                later = row >= k
                b = jnp.where(later, a * pltpu.roll(b, k, 0) + b, b)
                a = jnp.where(later, a * pltpu.roll(a, k, 0), a)
            h = a * carry[s] + b
            st[s, pl.ds(pl.multiple_of(8 + i * 8, 8), 8)] = h
            new.append(h[7:8])
        return tuple(new)

    last = lax.fori_loop(0, SEQ // 8, forward, (lru_before[0], lru_before[1]))
    saves.start(st, o_st)
    part[TOK:] = jnp.zeros((8, D), F32)
    part[TOK : TOK + 3, 0:RC] = u[1, PAD - 3 :]
    part[TOK + 3 : TOK + 4, 0:RC] = last[1]
    finals[0:3] = u[0, PAD - 3 :]
    finals[3:4] = last[0]

    @pl.loop(0, 6)
    def _(c):
        at = cols(c)
        act, _ = gelu_both(gate_in[:, at])
        for s in range(2):
            rows = slice(s * SEQ, (s + 1) * SEQ)
            merged[rows, at] = (st[s, 8:, at] * act[rows]).astype(BF16)

    saves.start(merged, o_merged)

    part[0:TOK] = nn(merged[...], wog[..., 0:D].reshape(RC, D))

    saves.wait()


def mlp_norm(tok, part, other, gains, normed2, own, o_residual, residual, sem):
    for s in range(2):
        rows, theirs = slice(s * SEQ, (s + 1) * SEQ), slice((1 - s) * SEQ, (2 - s) * SEQ)
        v = tok[rows].astype(F32) + (part[rows] + other[theirs])
        residual[rows] = v
        normed2[rows] = (v * inv_rms(v) * gains[1:2]).astype(BF16)
    copy = pltpu.make_async_copy(residual, o_residual, sem)
    copy.start()
    own[...] = residual[0:SEQ]
    copy.wait()


def mlp(
    places, cot, normed2, own, p0, p1, p2, p3, q0, q1, q2, q3,
    hidden, ggu, o_base, o_back,
    win, wdown, grad_hidden, down, back, base, sems, out_sems,
):
    for j, p in enumerate((p0, p1, p2, p3)):
        down_copy(p, places, j, wdown, sems.at[1])
    for j, (p, q) in enumerate(((p0, q0), (p1, q1), (p2, q2), (p3, q3))):
        p_copy(p, places, j, FC, PI, win, 0, sems.at[0])
        q_copy(q, places, j, 0, LATE, win, PI, sems.at[0])
    saves = Saves(out_sems)
    down[...] = jnp.zeros_like(down)
    back[...] = jnp.zeros_like(back)
    landed(wdown, sems.at[1])

    @pl.loop(0, 2)
    def _(c):
        grad_hidden[c] = nt(cot[...], wdown[c].reshape(768, D))

    landed(win, sems.at[0])

    @pl.loop(0, 2)
    def _(c):
        at = pl.ds(pl.multiple_of(768 * c, 256), 768)
        up = pl.ds(pl.multiple_of(FC + 768 * c, 256), 768)
        wa, wu = win[..., at].reshape(D, 768), win[..., up].reshape(D, 768)
        a = nn(normed2[...], wa)
        b = nn(normed2[...], wu)
        ga, da = gelu_both(a)
        h = (ga * b).astype(BF16)
        hidden[:, at] = h
        gh = grad_hidden[c]
        gg_a = (gh * b * da).astype(BF16)
        gg_b = (gh * ga).astype(BF16)
        ggu[:, at] = gg_a
        ggu[:, up] = gg_b
        down[...] += nn(h, wdown[c].reshape(768, D))
        back[...] += nt(gg_a, wa) + nt(gg_b, wu)

    saves.start(back, o_back.at[pl.ds(0, TOK)])
    saves.start(down.at[pl.ds(SEQ, SEQ)], o_back.at[pl.ds(TOK, SEQ)])
    base[...] = own[...] + down[0:SEQ]
    saves.start(base, o_base)
    saves.wait()


def emit(saves, block, places, axis, outs):
    for j in range(4):
        saves.start(block.at[places[4 + axis, j]], outs[j // 2].at[j % 2])


RINGS = [(x, z) for x in range(4) for z in range(4)]


def emit_columns(saves, block, places, axis, outs, first, count):
    for j in range(4):
        columns = pl.ds(first, count)
        saves.start(block.at[places[4 + axis, j], :, :, columns], outs[j // 2].at[j % 2, :, :, columns])


def mlp_grads(
    places, cot, normed2, hidden, ggu, p0, p1, q0, q1,
    bp, bq, out_sems,
):
    saves = Saves(out_sems)
    @pl.loop(0, 2)
    def _(xh):
        v = tn(hidden[:, pl.ds(pl.multiple_of(768 * xh, 256), 768)], cot[...]).astype(BF16)
        for z in range(4):
            for xl in range(2):
                r = 96 * (2 * z + xl)
                bp[2 * xh + xl, z, :, 0:D] = v[r : r + 64]
                bp[2 * xh + xl, z, 0:32, D:FC] = v[r + 64 : r + 96, 0:512]
                bp[2 * xh + xl, z, 32:64, D:FC] = v[r + 64 : r + 96, 512:1024]

    emit_columns(saves, bp, places, 0, (p0, p1), 0, FC)

    def put(block, order, first, to):
        v = tn(normed2[...], ggu[:, pl.ds(pl.multiple_of(first, 256), 768)]).astype(BF16)
        for x, z in RINGS:
            for half in range(2):
                r = ring_rows(x, z) + 256 * half
                at = (x, z) if order else (z, x)
                columns = pl.ds(pl.multiple_of(to, 256), 768)
                block[(*at, slice(32 * half, 32 * half + 32), columns)] = v[r : r + 32]

    put(bp, True, 0, FC)
    emit_columns(saves, bp, places, 0, (p0, p1), FC, PI)

    @pl.loop(0, 3)
    def _(part):
        put(bq, False, 768 * (part + 1), 768 * part)

    emit_columns(saves, bq, places, 2, (q0, q1), 0, LATE)
    saves.wait()


def rec_backward(
    places, tok, cot, masks, gains, chans, other, i_back, i_residual, i_normed, i_merged, i_u, i_gate, i_conv, i_rate,
    i_inp, i_st, i_tables, wp0, wp1, wp2, wp3, wq0, wq1, wq2, wq3,
    o_residual, o_mine, o_theirs, p0, p1, q0, q1,
    wb, wog, part, residual, normed, merged, u_in, gate_in, conv_low, rate, inp, st_in, tables,
    coeff, grad_branch, gs, lam, rate_low, inp_low, direct, gmix, rolled, sums, mixed_part, own_residual, bp, bq,
    sems, in_sems, out_sems,
):
    ins = Saves(in_sems)
    for source, target in (
        (i_back.at[pl.ds(0, TOK)], part), (i_residual, residual), (i_merged, merged), (i_gate, gate_in), (i_st, st_in),
        (i_rate, rate), (i_inp, inp), (i_conv, conv_low), (i_tables, tables), (i_u, u_in), (i_normed, normed),
    ):
        ins.start(source, target)
    for j, p in enumerate((wp0, wp1, wp2, wp3)):
        og_copy(p, places, j, wog, sems.at[1])
    for j, (p, q) in enumerate(((wp0, wq0), (wp1, wq1), (wp2, wq2), (wp3, wq3))):
        p_copy(p, places, j, OG, PB, wb, 0, sems.at[0])
        q_copy(q, places, j, 0, QB, wb, PB, sems.at[0])
    saves = Saves(out_sems)
    sums[...] = jnp.zeros_like(sums)
    for copy in ins.copies[0:2]:
        copy.wait()
    for s in range(2):
        rows, theirs = slice(s * SEQ, (s + 1) * SEQ), slice((1 - s) * SEQ, (2 - s) * SEQ)
        grad, term = rms_back(part[rows] + other[theirs], residual[rows], gains[1:2])
        grad = cot[rows].astype(F32) + grad
        grad_branch[rows] = grad.astype(BF16)
        if s == 0:
            own_residual[...] = grad
            sums[9:10] = jnp.sum(term, axis=0, keepdims=True)
    saves.start(own_residual, o_residual)

    def put_og(b, first, v):
        x, z = (b // 8) * 2 + b % 2, (b // 2) % 4
        n = min(max(OG - first, 0), v.shape[1])
        if n:
            bp[x, z, 0:48, first : first + n] = v[:, :n]
        if n < v.shape[1]:
            to = first + n - OG
            for r in range(3):
                bp[x, z, 48:64, 384 * r + to : 384 * r + to + v.shape[1] - n] = v[16 * r : 16 * r + 16, n:]

    ins.copies[2].wait()
    v = tn(merged[...], grad_branch[...]).astype(BF16)
    for b in range(16):
        put_og(b, 0, v[48 * b : 48 * b + 48])
    landed(wog, sems.at[1])
    gs[...] = nt(grad_branch[...], wog[..., 0:D].reshape(RC, D))
    for copy in ins.copies[3:5]:
        copy.wait()

    @pl.loop(0, 6)
    def _(c):
        at = cols(c)
        act, act_grad = gelu_both(gate_in[:, at])
        g = gs[:, at]
        for s in range(2):
            rows = slice(s * SEQ, (s + 1) * SEQ)
            gmix[rows, pl.ds(pl.multiple_of(RC + c * LANES, LANES), LANES)] = (
                g[rows] * st_in[s, 8:, at] * act_grad[rows]
            ).astype(BF16)
        gs[:, at] = g * act

    for copy in ins.copies[5:8]:
        copy.wait()

    @pl.loop(0, 6)
    def _(c):
        at = cols(c)
        keep, starts = masks[0], masks[1]
        rg = jax.nn.sigmoid(rate[:, at] + chans[5:6, at])
        sd = jnp.exp(-8.0 * rg * chans[7:8, at])
        coeff[:, at] = (1.0 - starts) * (keep * sd + (1.0 - keep))

    row = lax.broadcasted_iota(jnp.int32, (8, RC), 0)

    def backward(n, carry):
        i = SEQ // 8 - 1 - n
        new = []
        for s in range(2):
            at = pl.ds(pl.multiple_of(s * SEQ + i * 8, 8), 8)
            own = coeff[at]
            later_a, later_lam = carry[s]
            a = jnp.where(row == 7, later_a, pltpu.roll(own, 7, 0))
            b = gs[at]
            for k in (1, 2, 4):
                here = row < 8 - k
                b = jnp.where(here, b + a * pltpu.roll(b, 8 - k, 0), b)
                a = jnp.where(here, a * pltpu.roll(a, 8 - k, 0), a)
            h = b + a * later_lam
            lam[at] = h
            new.append((own[0:1], h[0:1]))
        return tuple(new)

    zero = jnp.zeros((1, RC), F32)
    lax.fori_loop(0, SEQ // 8, backward, ((zero, zero), (zero, zero)))

    @pl.loop(0, 6)
    def _(c):
        at = cols(c)
        decay = chans[7:8, at]
        for s in range(2):
            rows = slice(s * SEQ, (s + 1) * SEQ)
            keep, starts = masks[0, rows], masks[1, rows]
            rg, ig, sd, q, root, scale = gates(
                rate[rows, at], inp[rows, at], chans[5:6, at], chans[6:7, at], decay, keep, starts
            )
            conv = conv_low[rows, at].astype(F32)
            l = lam[rows, at]
            common = l * keep
            grad_coeff = l * st_in[s, 7 : PAD - 1, at]
            direct[rows, at] = common * scale * ig
            d_ig = common * scale * conv
            d_scale = common * ig * conv
            d_sd = (1.0 - starts) * (grad_coeff * keep - d_scale * jnp.where(q > 0.001, sd / root, 0.0))
            d_log = d_sd * sd * -8.0
            d_rate = d_log * decay * rg * (1.0 - rg)
            d_inp = d_ig * ig * (1.0 - ig)
            rate_low[rows, at] = d_rate.astype(BF16)
            inp_low[rows, at] = d_inp.astype(BF16)
            for n, term in ((5, d_rate), (6, d_inp), (7, d_log * rg)):
                sums[n : n + 1, at] += jnp.sum(term, axis=0, keepdims=True)

    for copy in ins.copies[8:]:
        copy.wait()
    turn = turn_matrix()
    top, left = quarter_masks()
    for p in range(2):
        at = slice(2 * HS * p, 2 * HS * (p + 1))
        direct[:, at] += nt(rate_low[:, at], tables[2 * p]) + nt(inp_low[:, at], tables[2 * p + 1])
        dr = tn(conv_low[:, at], rate_low[:, at]).astype(BF16)
        di = tn(conv_low[:, at], inp_low[:, at]).astype(BF16)
        none = jnp.zeros_like(dr)
        straight = jnp.where(top, jnp.where(left, dr, none), jnp.where(left, none, di))
        crossed = jnp.where(top, jnp.where(left, di, none), jnp.where(left, none, dr))
        g = (straight.astype(F32) + nn(crossed, turn)).astype(BF16)
        for b in range(8):
            put_og(8 * p + b, D, g[48 * b : 48 * b + 48])

    rolled[:, SEQ:] = jnp.zeros((2, 8, LANES), F32)

    @pl.loop(0, 6)
    def _(c):
        at = cols(c)
        for s in range(2):
            rows = slice(s * SEQ, (s + 1) * SEQ)
            g = direct[rows, at]
            gu = chans[0:1, at] * g
            sums[4:5, at] += jnp.sum(g, axis=0, keepdims=True)
            sums[0:1, at] += jnp.sum(g * u_in[s, 8:, at], axis=0, keepdims=True)
            for k in range(1, 4):
                w = g * masks[1 + k, rows]
                sums[k : k + 1, at] += jnp.sum(w * u_in[s, 8 - k : PAD - k, at], axis=0, keepdims=True)
                rolled[s, 0:SEQ] = w
                gu = gu + chans[k : k + 1, at] * rolled[s, k : SEQ + k]
            gmix[rows, at] = (gu * masks[0, rows]).astype(BF16)

    v = jnp.concatenate([sums[0:8, 0:RC], jnp.zeros((LANES - 8, RC), F32)], axis=0).T.astype(BF16)
    for b in range(16):
        put_og(b, 1408, v[48 * b : 48 * b + 48])
    landed(wb, sems.at[0])

    v = tn(normed[...], gmix[:, 0:PB]).astype(BF16)
    for x, z in RINGS:
        for half in range(2):
            r = ring_rows(x, z) + 256 * half
            bp[x, z, 32 * half : 32 * half + 32, OG:EARLY] = v[r : r + 32]
    emit(saves, bp, places, 0, (p0, p1))
    mixed_part[...] = nt(gmix[...], rows_of(wb, 0, BRANCH))
    saves.start(mixed_part.at[pl.ds(0, SEQ)], o_mine)
    saves.start(mixed_part.at[pl.ds(SEQ, SEQ)], o_theirs)
    t = tok[...].astype(F32)
    sums[8:9] = jnp.sum(mixed_part[...] * (t * inv_rms(t)), axis=0, keepdims=True)
    v = jnp.concatenate([sums[8:16], jnp.zeros((LANES - 8, D), F32)], axis=0).T.astype(BF16)
    for x, z in RINGS:
        for half in range(2):
            r = ring_rows(x, z) + 256 * half
            bq[z, x, 32 * half : 32 * half + 32, QB:EARLY] = v[r : r + 32]

    v = tn(normed[...], gmix[:, PB:]).astype(BF16)
    for x, z in RINGS:
        for half in range(2):
            r = ring_rows(x, z) + 256 * half
            bq[z, x, 32 * half : 32 * half + 32, 0:QB] = v[r : r + 32]
    emit(saves, bq, places, 2, (q0, q1))
    saves.wait()


def join_sums(
    places, eo_p, eu_p, lo_p, lu_p, eo_q, eu_q, lo_q, lu_q,
    p0, p1, q0, q1,
    out, out_sems,
):
    saves = Saves(out_sems)
    for n, (axis, outs, a, b, c, d) in enumerate(
        ((2, (p0, p1), eo_p, eu_p, lo_p, lu_p), (0, (q0, q1), eo_q, eu_q, lo_q, lu_q))
    ):
        for j in range(4):
            at, to = places[4 + axis, j], 4 * n + j
            out[to, :, 0:EARLY] = add(a[at], b[at])
            out[to, :, EARLY:] = add(c[at], d[at])
            saves.start(out.at[to], outs[j // 2].at[j % 2])
    saves.wait()


def add(a, b):
    return (a.astype(F32) + b.astype(F32)).astype(BF16)


def half_sums(a_p, b_p, c_p, d_p, a_q, b_q, c_q, d_q, *rest):
    outs, (early, late, in_sems) = rest[-7:-3], rest[-3:]
    loads = Saves(in_sems)
    for n, (a, b, c, d) in enumerate(((a_p, b_p, c_p, d_p), (a_q, b_q, c_q, d_q))):
        for source, target in ((a, early.at[n, 0]), (b, early.at[n, 1]), (c, late.at[n, 0]), (d, late.at[n, 1])):
            loads.start(source.at[0], target)
    for n in range(2):
        for i, v in enumerate((early, late)):
            loads.copies[4 * n + 2 * i].wait()
            loads.copies[4 * n + 2 * i + 1].wait()
            outs[2 * n + i][...] = add(v[n, 0], v[n, 1])


def pass_on(a_p, f_p, a_q, f_q, *rest):
    o_p, o_q, v, in_sems, out_sems = rest[-5:]
    loads, saves = Saves(in_sems), Saves(out_sems)
    for i, source in enumerate((a_p, f_p, a_q, f_q)):
        loads.start(source.at[1], v.at[i])
    for n, out in enumerate((o_p, o_q)):
        loads.copies[2 * n].wait()
        loads.copies[2 * n + 1].wait()
        v[2 * n] = add(v[2 * n], v[2 * n + 1])
        saves.start(v.at[2 * n], out)
    saves.wait()


def cut(
    places, p0, p1, p2, q0, q1, q2,
    o0, o1, o2, o3,
    parts, sp, sq, sd, in_sems,
):
    load((p0.at[0], p1.at[0], p2, q0.at[0], q1.at[0], q2), [parts.at[i] for i in range(6)], in_sems)
    for n, out in enumerate((sp, sq)):
        out[...] = parts[3 * n].astype(F32) + parts[3 * n + 1].astype(F32) + parts[3 * n + 2].astype(F32)
    sd[0:64] = sp[:, EARLY : EARLY + D]
    sd[64:96, 0:512] = sp[0:32, EARLY + D : EARLY + FC]
    sd[64:96, 512:1024] = sp[32:64, EARLY + D : EARLY + FC]
    tail = jnp.concatenate([sp[48:64, 384 * r : 384 * r + 384] for r in range(3)], axis=0)
    og = jnp.concatenate([sp[0:48, 0:OG], tail], axis=1).astype(BF16)
    i = lax.broadcasted_iota(jnp.int32, (16, 48), 0)
    s = lax.broadcasted_iota(jnp.int32, (16, 48), 1)

    def two(rows):
        return jnp.concatenate(rows, axis=0).astype(BF16)

    for j, out in enumerate((o0, o1, o2, o3)):
        y = places[1, (0, 2, 3, 1)[j]]
        rows = [pl.ds(pl.multiple_of(32 * c + y * 8, 8), 8) for c in range(2)]
        out[:, 0:PB] = two([sp[r, OG:EARLY] for r in rows])
        out[:, PB : PB + PI] = two([sp[r, UNIT - PI :] for r in rows])
        out[:, PB + PI : DC] = two([sq[r] for r in rows])
        mine = jnp.where((s == i + y * 12) & (i < 12), 1.0, 0.0).astype(BF16)
        out[:, DC:DOWN] = nn(mine, og).astype(BF16)
        down = sd[pl.ds(pl.multiple_of(y * 24, 8), 24)]
        out[:, DOWN : DOWN + D] = down[0:16].astype(BF16)
        out[:, DOWN + D :] = two([down[16:24, 0:512], down[16:24, 512:]])


def finish(places, o0, o1, o2, o3, mine, theirs, out_grad, gate_grad, chan_grad, down_grad, v):
    v[...] = o0[...].astype(F32) + o1[...].astype(F32) + o2[...].astype(F32) + o3[...].astype(F32)
    core = places[3, 0]
    theirs[...] = v[pl.ds(pl.multiple_of((1 - core) * 8, 8), 8), 0:DC]
    mine[...] = v[pl.ds(pl.multiple_of(core * 8, 8), 8), 0:DC]
    out_grad[...] = v[0:12, DC : DC + D]
    gate_grad[...] = v[0:12, DC + D : DC + D + 384]
    chan_grad[...] = v[:, DC + D + 384 : DOWN].T[0:8]
    down_grad[0:16] = v[:, DOWN : DOWN + D]
    down_grad[16:24, 0:512] = v[0:8, DOWN + D :]
    down_grad[16:24, 512:] = v[8:16, DOWN + D :]


def unpack(places, mine, theirs, branch, inner, gains):
    def halves(ins):
        for c, v in enumerate(ins):
            for q in range(4):
                to = 768 * q + 384 * c
                if q == 0:
                    branch[:, to : to + PB] = v[:, 0:PB]
                    branch[:, to + PB : to + 384] = v[:, PB + PI : PB + PI + 128]
                else:
                    branch[:, to : to + 384] = v[:, PI + 384 * q : PI + 384 * q + 384]
                at = PB if q == 0 else DC - LATE + 768 * (q - 1)
                to = 1536 * q + 768 * c
                inner[:, to : to + 768] = v[:, at : at + 768]

    gains[...] = mine[:, DC - LATE - LANES : DC - LATE] + theirs[:, DC - LATE - LANES : DC - LATE]

    @pl.when(places[3, 0] == 0)
    def _():
        halves((mine, theirs))

    @pl.when(places[3, 0] == 1)
    def _():
        halves((theirs, mine))


VM, HB, SM, ANY = pltpu.VMEM, pltpu.HBM, pltpu.SMEM, pl.ANY


def kernel(body, ins, spaces, outs, scratch, mib, flops=0, aliases={}):
    moved = sum(v.size * v.dtype.itemsize for v in ins)
    ins = [pltpu.with_memory_space_constraint(v, HB) if s is HB else v for v, s in zip(ins, spaces)]
    return pl.pallas_call(
        body,
        out_shape=[HB(s, d) if at is HB else jax.ShapeDtypeStruct(s, d) for s, d, at in outs],
        in_specs=[pl.BlockSpec(memory_space=s) for s in spaces],
        out_specs=[pl.BlockSpec(memory_space=s) for _, _, s in outs],
        scratch_shapes=scratch,
        input_output_aliases=aliases,
        compiler_params=pltpu.CompilerParams(vmem_limit_bytes=mib * 2**20),
        cost_estimate=pl.CostEstimate(flops=flops, bytes_accessed=moved, transcendentals=0),
    )(*ins)


def shards(
    tokens, cotangent, segment, keep_mask, conv_state, lru_state, norm1_gain, conv_weight, lru_bias, decay_rate,
    gate_weight, branch_weight, out_weight, norm2_gain, mlp_in_weight, mlp_out_weight,
):
    here = my_place()
    core = here["core"]
    zero = jnp.zeros_like(core)
    places = jnp.stack(
        [jnp.stack(ring_places(axis, here)) for axis in "xyz"]
        + [jnp.stack([core, zero, zero, zero])]
        + [jnp.stack(pair_places(axis, here)) for axis in "xyz"]
    ).astype(jnp.int32)
    vmem, dma = pltpu.VMEM, pltpu.SemaphoreType.DMA

    tc = jnp.concatenate([tokens[0], cotangent[0]], axis=0)
    tc_other = swap(tc)
    marks = jnp.concatenate([segment, keep_mask], axis=1).astype(F32)
    states = jnp.concatenate([conv_state[0], lru_state], axis=0)
    sent = jnp.concatenate([core_half(states, 1 - core, 2), jnp.pad(marks, ((0, 0), (0, RC - 2 * SEQ)))], axis=0)
    sent = swap(sent)

    mine, theirs, own = kernel(
        pack,
        (places, branch_weight, mlp_in_weight, jnp.stack([norm1_gain, norm2_gain]), out_weight, gate_weight,
         jnp.concatenate([conv_weight, lru_bias, decay_rate[None]], axis=0), mlp_out_weight),
        [SM, HB, HB, VM, HB, HB, VM, HB],
        [((8, DC), BF16, VM)] * 2 + [((16, OWN - DC), BF16, VM)],
        [vmem(v.shape, BF16) for v in (branch_weight, mlp_in_weight, out_weight, gate_weight, mlp_out_weight)]
        + [dma((5,))],
        8,
    )
    (block,) = kernel(join, (places, mine, swap(theirs), own), [SM] + [VM] * 3, [((16, OWN), BF16, VM)], [], 8)

    row = ((64, UNIT), BF16)
    unit_of = ((2, 32, UNIT), BF16)
    p, q = kernel(
        unit,
        (places, *ring_direct(block, "y"), tc_other, sent),
        [SM] + [VM] * 4 + [ANY] * 2,
        [(*unit_of, HB)] * 2,
        [vmem(*row), vmem(*row), vmem((64, DC), F32), vmem((96, D), F32), dma((4,))],
        16,
    )
    early, late = (4, 64, EARLY), (4, 64, LATE)
    stack = ((4, 64, UNIT), BF16)
    p, q = ring_both(p, "z"), ring_both(q, "x")
    stacks = [((*v, n), BF16, HB) for n in (EARLY, LATE) for v in ((2, 4, 32), (2, 2, 2, 32))]
    unit_of = (2, 32, UNIT)
    partial = kernel(
        planes((0, 1, 2)),
        (places, *p[:3], *q[:3]),
        [SM] + [HB] * 6,
        stacks,
        [vmem((6, *unit_of), BF16), dma((6,)), dma((12,))],
        8,
    )
    pe, qe, pl_, ql = kernel(
        planes((3,)),
        (places, p[3], q[3], *partial),
        [SM, ANY, ANY] + [HB] * 4,
        stacks,
        [vmem((2, *unit_of), BF16), dma((2,)), dma((4,))],
        8,
        aliases={3 + i: i for i in range(4)},
    )
    pe, qe, pl_, ql = ring_both(pe, "x"), ring_both(qe, "z"), ring_both(pl_, "x"), ring_both(ql, "z")

    tok = jnp.concatenate([tc[:SEQ], tc_other[:SEQ]], axis=0)
    cot = jnp.concatenate([tc[SEQ:], tc_other[SEQ:]], axis=0)
    states = jnp.stack([core_half(states, core, 2), sent[:4]])
    marks = jnp.concatenate([marks, sent[4:, : 2 * SEQ]], axis=0)
    seg, keep = marks[:, :SEQ], marks[:, SEQ:]
    earlier = [jnp.concatenate([jnp.repeat(seg[:, :1], k, axis=1), seg[:, : SEQ - k]], axis=1) for k in range(1, 4)]
    masks = jnp.stack([keep, (earlier[0] != seg).astype(F32)] + [(e == seg).astype(F32) for e in earlier])
    masks = jnp.broadcast_to(masks.reshape(5, TOK, 1), (5, TOK, LANES))

    wide, wide_low = ((TOK, D), F32), ((TOK, D), BF16)
    act, act_low, padded = ((TOK, RC), F32), ((TOK, RC), BF16), ((2, PAD, RC), F32)
    tables = ((4, 2 * HS, 2 * HS), BF16)
    saved = [wide_low, act_low, padded, act, act_low, act, act, padded, tables]
    part, finals, gains, chans, normed, merged, u, gate_in, conv_low, rate, inp, st, table = kernel(
        rec_forward,
        (places, tok, masks, states[:, :3], states[:, 3:], *pe, *qe),
        [SM] + [VM] * 4 + [HB] * 8,
        [((TOK + 8, D), F32, VM), ((4, RC), F32, VM), ((8, D), F32, VM), ((8, RC), F32, VM)]
        + [(*v, HB) for v in saved],
        [vmem((*ROWS, PB + EARLY), BF16), vmem((*OG_ROWS, OGC), BF16)]
        + [vmem(*v) for v in saved + [act, act]]
        + [dma((2,)), dma((9,))],
        32,
        2 * TOK * (D * BRANCH + RC * (D + 768)),
    )
    half = ((SEQ, D), F32)
    other = swap(part)
    normed2, own, residual = kernel(
        mlp_norm,
        (tok, part, other, gains),
        [VM] * 4,
        [(*wide_low, VM), (*half, VM), (*wide, HB)],
        [vmem(*wide), dma],
        16,
    )
    hidden, ggu, base, back = kernel(
        mlp,
        (places, cot, normed2, own, *pl_, *ql),
        [SM] + [VM] * 3 + [ANY] * 8,
        [((TOK, FC), BF16, VM), ((TOK, INNER), BF16, VM), (*half, HB), ((TOK + SEQ, D), F32, HB)],
        [vmem((*ROWS, INNER), BF16), vmem((*DOWN_ROWS, D), BF16), vmem((2, TOK, 768), F32)]
        + [vmem(*v) for v in (wide, wide, half)]
        + [dma((2,)), dma((3,))],
        32,
        2 * TOK * D * (2 * INNER + 2 * FC),
    )
    back_other = swap(back)
    outs = kernel(
        mlp_grads,
        (places, cot, normed2, hidden, ggu),
        [SM] + [VM] * 4,
        [((2, *late), BF16, HB)] * 4,
        [vmem((4,) + late, BF16), vmem((4,) + late, BF16), dma((12,))],
        32,
        2 * TOK * D * (INNER + FC),
    )
    lp, lq = outs[:2], outs[2:]

    def first_half(p, q, routes):
        return send(p[1], partner(routes[0], 0)), send(q[1], partner(routes[1], 0))

    def second_half(p, q, came, routes, shape, until=(), lands=HB):
        up = kernel(
            pass_on,
            (p[0], came[0], q[0], came[1], *until),
            [HB, lands, HB, lands] + [HB] * len(until),
            [(shape, BF16, HB)] * 2,
            [vmem((4,) + shape, BF16), dma((4,)), dma((2,))],
            16,
        )
        return send(up[0], partner(routes[0], 1)), send(up[1], partner(routes[1], 1))

    late_came = first_half(lp, lq, "xz")
    outs = kernel(
        rec_backward,
        (places, tok, cot, masks, gains, chans, back_other, back, residual, normed, merged, u, gate_in, conv_low, rate,
         inp, st, table, *pe, *qe),
        [SM] + [VM] * 6 + [HB] * 19,
        [(*v, HB) for v in (half, half, half)] + [((2, *early), BF16, HB)] * 4,
        [vmem((*ROWS, BRANCH), BF16), vmem((*OG_ROWS, OGC), BF16)]
        + [vmem(*v) for v in (wide, wide, wide_low, act_low, padded, act, act_low, act, act, padded, tables)]
        + [vmem(*v) for v in (act, wide_low, act, act, act_low, act_low, act, ((TOK, BRANCH), BF16))]
        + [vmem((2, PAD, LANES), F32), vmem((16, D), F32), vmem(*wide), vmem(*half)]
        + [vmem((4,) + early, BF16), vmem((4,) + early, BF16), dma((2,)), dma((11,)), dma((11,))],
        48,
        2 * TOK * D * (2 * BRANCH + 2 * RC),
    )
    grad_residual, mixed_mine, mixed_theirs = outs[:3]
    ep, eq = outs[3:5], outs[5:]
    early_came = first_half(ep, eq, "xz")
    late_up = second_half(lp, lq, late_came, "xz", late, (ep[0],))
    early_up = second_half(ep, eq, early_came, "xz", early)

    summed = kernel(
        half_sums,
        (ep[0], early_came[0], lp[0], late_came[0], eq[0], early_came[1], lq[0], late_came[1]),
        [HB] * 8,
        [(early, BF16, VM), (late, BF16, VM)] * 2,
        [vmem((2, 2) + early, BF16), vmem((2, 2) + late, BF16), dma((8,))],
        16,
    )
    outs = kernel(
        join_sums,
        (places, summed[0], early_up[0], summed[1], late_up[0], summed[2], early_up[1], summed[3], late_up[1]),
        [SM] + [VM] * 8,
        [((2, 64, UNIT), BF16, HB)] * 4,
        [vmem((8, 64, UNIT), BF16), dma((8,))],
        8,
    )
    tp, tq = outs[:2], outs[2:]
    came = first_half(tp, tq, "zx")
    up = second_half(tp, tq, came, "zx", (64, UNIT), lands=ANY)
    sums = kernel(
        cut,
        (places, tp[0], came[0], up[0], tq[0], came[1], up[1]),
        [SM] + [HB, ANY, ANY] * 2,
        [((16, OWN), BF16, VM)] * 4,
        [vmem((6, 64, UNIT), BF16), vmem((64, UNIT), F32), vmem((64, UNIT), F32), vmem((96, D), F32), dma((6,))],
        16,
    )
    mine, theirs, out_grad, gate_grad, chan_grad, down_grad = kernel(
        finish,
        (places, *terms_direct(sums, "y")),
        [SM] + [VM] * 4,
        [((8, DC), F32, VM)] * 2 + [(s, F32, VM) for s in ((12, D), (12, 384), (8, 16), (24, D))],
        [vmem((16, OWN), F32)],
        8,
    )
    branch_grad, in_grad, gain_grads = kernel(
        unpack,
        (places, mine, swap(theirs)),
        [SM] + [VM] * 2,
        [((8, 2 * R), F32, VM), ((8, 2 * F), F32, VM), ((8, LANES), F32, VM)],
        [],
        8,
    )

    output = (base + back_other[TOK:]).astype(BF16)
    grad, _ = rms_back(mixed_mine + swap(mixed_theirs), tok[:SEQ].astype(F32), gains[0])
    input_grad = (grad_residual + grad).astype(BF16)
    theirs = other[TOK : TOK + 4, :RC]
    finals = jnp.stack(
        [v.reshape(1, 4, 2, 384) for v in (jnp.where(core == 0, finals, theirs), jnp.where(core == 0, theirs, finals))],
        axis=3,
    ).reshape(1, 4, R)
    return (
        output[None],
        input_grad[None],
        finals[:, :3],
        finals[:, 3],
        gain_grads[:, 0],
        chan_grad[:4, :12],
        chan_grad[4:7, :12],
        chan_grad[7, :12],
        gate_grad,
        branch_grad,
        out_grad,
        gain_grads[:, 1],
        in_grad,
        down_grad,
    )


def solution(mesh):
    rows, last = P(AXES), P(None, AXES)
    specs = [rows] * 6 + [rows, last, last] + [rows] * 7
    outs = [rows] * 4 + [rows, last, last] + [rows] * 7
    return jax.shard_map(
        shards, mesh=mesh, in_specs=tuple(specs), out_specs=tuple(outs), check_vma=False
    )
```

profile of v0, /device:TPU:0, one launch (start us, length us, event | category | flops | bytes accessed | tf_op | source)
XLA Modules:
  0.0 262.2 jit_solution(11035064423480866207)
XLA Ops:
  7.1 3.4 %collective-permute-start.5 = (bf16[16,7808]{1,0:T(8,128)(2,1)S(1)}, bf16[16,7808]{1,0:T(8,128)(2,1)S(1)}, u32[]{:S(2)}, u32[]{:S(2)}) collective-permute-start(bf16[16,7808]{1,0:T(8,128)(2,1)S(1)} %shard_map.264.p0), channel_id=1, source_target_pairs={{0,2},{1,3},{2,0},{3,1},{4,6},{5,7},{6,4},{7,5},{8,10},{9,11},{10,... | collective-permute-start | bytes 749576 | tf_op jit(solution)/shard_map/ppermute | solution.py:66
  13.9 3.7 %collective-permute-done.5.p3 = bf16[16,7808]{1,0:T(8,128)(2,1)S(1)} collective-permute-done((bf16[16,7808]{1,0:T(8,128)(2,1)S(1)}, bf16[16,7808]{1,0:T(8,128)(2,1)S(1)}, u32[]{:S(2)}, u32[]{:S(2)}) %collective-permute-start.5) | collective-permute-done | bytes 249888 | tf_op jit(solution)/shard_map/ppermute | solution.py:66
  17.6 4.9 %collective-permute-done.4.p2 = bf16[16,7808]{1,0:T(8,128)(2,1)S(1)} collective-permute-done((bf16[16,7808]{1,0:T(8,128)(2,1)S(1)}, bf16[16,7808]{1,0:T(8,128)(2,1)S(1)}, u32[]{:S(2)}, u32[]{:S(2)}) %collective-permute-start.4) | collective-permute-done | bytes 249888 | tf_op jit(solution)/shard_map/ppermute | solution.py:66
  31.7 4.6 %collective-permute-done.6.refs_1_ = bf16[2,32,3712]{2,1,0:T(8,128)(2,1)S(1)} collective-permute-done((bf16[2,32,3712]{2,1,0:T(8,128)(2,1)}, bf16[2,32,3712]{2,1,0:T(8,128)(2,1)S(1)}, u32[]{:S(2)}, u32[]{:S(2)}) %collective-permute-start.6) | collective-permute-done | bytes 475168 | tf_op jit(solution)/shard_map/ppermute | solution.py:66
  41.7 3.4 %shard_map.266 = (bf16[2,4,32,1408]{3,2,1,0:T(8,128)(2,1)}, bf16[2,2,2,32,1408]{4,3,2,1,0:T(8,128)(2,1)}, bf16[2,4,32,2304]{3,2,1,0:T(8,128)(2,1)}, bf16[2,2,2,32,2304]{4,3,2,1,0:T(8,128)(2,1)}) custom-call(s32[7,4]{1,0:T(8,128)S(1)} %stack.185.places, bf16[2,32,3712]{2,1,0:T(8,128)(2,1)} %get-tuple-element.88.refs_0_, bf16[2,32,3712]{2,1,0:T(8,128)(2,1)} %copy-done.16, ...), custom_call_target="tpu_custom_call" | custom-call | bytes 2850928 | tf_op jit(solution)/shard_map/pallas_call | solution.py:915
  45.1 2.8 %collective-permute-done.7.refs_0_ = bf16[2,32,3712]{2,1,0:T(8,128)(2,1)S(1)} collective-permute-done((bf16[2,32,3712]{2,1,0:T(8,128)(2,1)S(1)}, bf16[2,32,3712]{2,1,0:T(8,128)(2,1)S(1)}, u32[]{:S(2)}, u32[]{:S(2)}) %collective-permute-start.7) | collective-permute-done | bytes 475168 | tf_op jit(solution)/shard_map/ppermute | solution.py:66
  53.2 3.6 %collective-permute-start.15 = (bf16[2,2,2,32,1408]{4,3,2,1,0:T(8,128)(2,1)}, bf16[2,2,2,32,1408]{4,3,2,1,0:T(8,128)(2,1)}, u32[]{:S(2)}, u32[]{:S(2)}) collective-permute-start(bf16[2,2,2,32,1408]{4,3,2,1,0:T(8,128)(2,1)} %get-tuple-element.95.q0.wq0), channel_id=1, source_target_pairs={{0,8},{1,9},{2,10},{3,11},{4,12},{5,13},{6,14},{7,15},{8,16},{9,17... | collective-permute-start | bytes 2162696 | tf_op jit(solution)/shard_map/ppermute | solution.py:66
  59.0 11.4 %collective-permute-done.13.p2.wp2 = bf16[2,4,32,1408]{3,2,1,0:T(8,128)(2,1)} collective-permute-done((bf16[2,4,32,1408]{3,2,1,0:T(8,128)(2,1)}, bf16[2,4,32,1408]{3,2,1,0:T(8,128)(2,1)}, u32[]{:S(2)}, u32[]{:S(2)}) %collective-permute-start.13) | collective-permute-done | bytes 720928 | tf_op jit(solution)/shard_map/ppermute | solution.py:66
  74.4 17.0 %collective-permute-done.16.q2.wq2 = bf16[2,2,2,32,1408]{4,3,2,1,0:T(8,128)(2,1)S(1)} collective-permute-done((bf16[2,2,2,32,1408]{4,3,2,1,0:T(8,128)(2,1)}, bf16[2,2,2,32,1408]{4,3,2,1,0:T(8,128)(2,1)S(1)}, u32[]{:S(2)}, u32[]{:S(2)}) %collective-permute-start.16) | collective-permute-done | bytes 720928 | tf_op jit(solution)/shard_map/ppermute | solution.py:66
  95.6 5.1 %collective-permute-done.17.q3.wq3 = bf16[2,2,2,32,1408]{4,3,2,1,0:T(8,128)(2,1)S(1)} collective-permute-done((bf16[2,2,2,32,1408]{4,3,2,1,0:T(8,128)(2,1)}, bf16[2,2,2,32,1408]{4,3,2,1,0:T(8,128)(2,1)S(1)}, u32[]{:S(2)}, u32[]{:S(2)}) %collective-permute-start.17) | collective-permute-done | bytes 720928 | tf_op jit(solution)/shard_map/ppermute | solution.py:66
  101.6 8.6 %shard_map.268 = (f32[264,1024]{1,0:T(8,128)S(1)}, f32[4,768]{1,0:T(4,128)S(1)}, f32[8,1024]{1,0:T(8,128)S(1)}, f32[8,768]{1,0:T(8,128)S(1)}, bf16[256,1024]{1,0...) custom-call(s32[7,4]{1,0:T(8,128)S(1)} %stack.185.places, ...), custom_call_target="tpu_custom_call" | custom-call | flops 1509949440 | bytes 6971504 | tf_op jit(solution)/shard_map/pallas_call | solution.py:915
  115.7 2.9 %collective-permute-done.23.q2 = bf16[2,2,2,32,2304]{4,3,2,1,0:T(8,128)(2,1)S(1)} collective-permute-done((bf16[2,2,2,32,2304]{4,3,2,1,0:T(8,128)(2,1)}, bf16[2,2,2,32,2304]{4,3,2,1,0:T(8,128)(2,1)S(1)}, u32[]{:S(2)}, u32[]{:S(2)}) %collective-permute-start.23) | collective-permute-done | bytes 1179680 | tf_op jit(solution)/shard_map/ppermute | solution.py:66
  119.3 9.2 %shard_map.270 = (bf16[256,1536]{1,0:T(8,128)(2,1)S(1)}, bf16[256,3072]{1,0:T(8,128)(2,1)S(1)}, f32[128,1024]{1,0:T(8,128)}, f32[384,1024]{1,0:T(8,128)}) custom-call(s32[7,4]{1,0:T(8,128)S(1)} %stack.185.places, bf16[256,1024]{1,0:T(8,128)(2,1)S(1)} %pad_maximum_fusion.2.cot, bf16[256,1024]{1,0:T(8,128)(2,1)S(1)} %get-tuple-element.98.normed2, ...), custom_call_target="tpu_custom_call" | custom-call | flops 4831838208 | bytes 11010160 | tf_op jit(solution)/shard_map/pallas_call | solution.py:915
  128.6 6.6 %shard_map.272 = (bf16[2,4,64,2304]{3,2,1,0:T(8,128)(2,1)}, bf16[2,4,64,2304]{3,2,1,0:T(8,128)(2,1)}, bf16[2,4,64,2304]{3,2,1,0:T(8,128)(2,1)}, bf16[2,4,64,2304]{3,2,1,0:T(8,128)(2,1)}) custom-call(s32[7,4]{1,0:T(8,128)S(1)} %stack.185.places, bf16[256,1024]{1,0:T(8,128)(2,1)S(1)} %pad_maximum_fusion.2.cot, ...), custom_call_target="tpu_custom_call" | custom-call | flops 2415919104 | bytes 3407984 | tf_op jit(solution)/shard_map/pallas_call | solution.py:915
  138.0 15.9 %shard_map.271 = (f32[128,1024]{1,0:T(8,128)}, f32[128,1024]{1,0:T(8,128)}, f32[128,1024]{1,0:T(8,128)}, bf16[2,4,64,1408]{3,2,1,0:T(8,128)(2,1)}, bf16[2,4,64,1...) custom-call(s32[7,4]{1,0:T(8,128)S(1)} %stack.185.places, ...), custom_call_target="tpu_custom_call" | custom-call | flops 2415919104 | bytes 18243696 | tf_op jit(solution)/shard_map/pallas_call | solution.py:915
  155.7 8.6 %collective-permute-done.28.d_p.f_p = bf16[2,4,64,2304]{3,2,1,0:T(8,128)(2,1)S(1)} collective-permute-done((bf16[2,4,64,2304]{3,2,1,0:T(8,128)(2,1)}, bf16[2,4,64,2304]{3,2,1,0:T(8,128)(2,1)S(1)}, u32[]{:S(2)}, u32[]{:S(2)}) %collective-permute-start.28) | collective-permute-done | bytes 2359328 | tf_op jit(solution)/shard_map/ppermute | solution.py:66
  166.7 3.7 %shard_map.275 = (bf16[4,64,2304]{2,1,0:T(8,128)(2,1)}, bf16[4,64,2304]{2,1,0:T(8,128)(2,1)}) custom-call(bf16[2,4,64,2304]{3,2,1,0:T(8,128)(2,1)} %get-tuple-element.123.c_p.a_p, bf16[2,4,64,2304]{3,2,1,0:T(8,128)(2,1)} %copy-done.3, bf16[2,4,64,2304]{3,2,1,0:T(8,128)(2,1)} %get-tuple-element.127.c_q.a_q, bf16[2,4,64,2304]{3,2,1,0:T(8,128)(2,1)} %copy-done.4, ...), custom_call_target="tpu_custom_call" | custom-call | bytes 10878976 | tf_op jit(solution)/shard_map/pallas_call | solution.py:915
  170.4 3.0 %collective-permute-start.32 = (bf16[4,64,2304]{2,1,0:T(8,128)(2,1)}, bf16[4,64,2304]{2,1,0:T(8,128)(2,1)S(1)}, u32[]{:S(2)}, u32[]{:S(2)}) collective-permute-start(bf16[4,64,2304]{2,1,0:T(8,128)(2,1)} %get-tuple-element.132), channel_id=1, source_target_pairs={{0,68},{1,69},{2,70},{3,71},{4,64},{5,65},{6,66},{7,67},{8,76},{9,... | collective-permute-start | bytes 3538952 | tf_op jit(solution)/shard_map/ppermute | solution.py:66
  174.7 9.0 %collective-permute-done.27.b_p.f_p = bf16[2,4,64,1408]{3,2,1,0:T(8,128)(2,1)S(1)} collective-permute-done((bf16[2,4,64,1408]{3,2,1,0:T(8,128)(2,1)}, bf16[2,4,64,1408]{3,2,1,0:T(8,128)(2,1)S(1)}, u32[]{:S(2)}, u32[]{:S(2)}) %collective-permute-start.27) | collective-permute-done | bytes 1441824 | tf_op jit(solution)/shard_map/ppermute | solution.py:66
  187.5 2.8 %shard_map.274 = (bf16[4,64,1408]{2,1,0:T(8,128)(2,1)}, bf16[4,64,1408]{2,1,0:T(8,128)(2,1)}) custom-call(bf16[2,4,64,1408]{3,2,1,0:T(8,128)(2,1)} %get-tuple-element.119.a_p.rest_0_, bf16[2,4,64,1408]{3,2,1,0:T(8,128)(2,1)} %copy-done.7, bf16[2,4,64,1408]{3,2,1,0:T(8,128)(2,1)} %get-tuple-element.125.a_q, bf16[2,4,64,1408]{3,2,1,0:T(8,128)(2,1)} %copy-done.8), custom_call_target="tpu_custom_call" | custom-call | bytes 5767168 | tf_op jit(solution)/shard_map/pallas_call | solution.py:915
  190.3 3.4 %collective-permute-start.31 = (bf16[4,64,1408]{2,1,0:T(8,128)(2,1)}, bf16[4,64,1408]{2,1,0:T(8,128)(2,1)S(1)}, u32[]{:S(2)}, u32[]{:S(2)}) collective-permute-start(bf16[4,64,1408]{2,1,0:T(8,128)(2,1)} %get-tuple-element.130), channel_id=1, source_target_pairs={{0,68},{1,69},{2,70},{3,71},{4,64},{5,65},{6,66},{7,67},{8,76},{9,... | collective-permute-start | bytes 2162696 | tf_op jit(solution)/shard_map/ppermute | solution.py:66
  196.0 3.5 %shard_map.273 = (bf16[4,64,1408]{2,1,0:T(8,128)(2,1)S(1)}, bf16[4,64,2304]{2,1,0:T(8,128)(2,1)S(1)}, bf16[4,64,1408]{2,1,0:T(8,128)(2,1)S(1)}, bf16[4,64,2304]{2,1,0:T(8,128)(2,1)S(1)}) custom-call(bf16[2,4,64,1408]{3,2,1,0:T(8,128)(2,1)} %get-tuple-element.119.a_p.rest_0_, bf16[2,4,64,1408]{3,2,1,0:T(8,128)(2,1)} %copy-done.7, ...), custom_call_target="tpu_custom_call" | custom-call | bytes 15204352 | tf_op jit(solution)/shard_map/pallas_call | solution.py:915
  199.6 3.6 %collective-permute-done.31.eu_p = bf16[4,64,1408]{2,1,0:T(8,128)(2,1)S(1)} collective-permute-done((bf16[4,64,1408]{2,1,0:T(8,128)(2,1)}, bf16[4,64,1408]{2,1,0:T(8,128)(2,1)S(1)}, u32[]{:S(2)}, u32[]{:S(2)}) %collective-permute-start.31) | collective-permute-done | bytes 720928 | tf_op jit(solution)/shard_map/ppermute | solution.py:66
  203.2 3.3 %collective-permute-done.33.eu_q = bf16[4,64,1408]{2,1,0:T(8,128)(2,1)} collective-permute-done((bf16[4,64,1408]{2,1,0:T(8,128)(2,1)}, bf16[4,64,1408]{2,1,0:T(8,128)(2,1)}, u32[]{:S(2)}, u32[]{:S(2)}) %collective-permute-start.33) | collective-permute-done | bytes 720928 | tf_op jit(solution)/shard_map/ppermute | solution.py:66
  206.5 3.6 %shard_map.276 = (bf16[2,64,3712]{2,1,0:T(8,128)(2,1)}, bf16[2,64,3712]{2,1,0:T(8,128)(2,1)}, bf16[2,64,3712]{2,1,0:T(8,128)(2,1)}, bf16[2,64,3712]{2,1,0:T(8,128)(2,1)}) custom-call(s32[7,4]{1,0:T(8,128)S(1)} %stack.185.places, bf16[4,64,1408]{2,1,0:T(8,128)(2,1)S(1)} %get-tuple-element.129.eo_p, bf16[4,64,1408]{2,1,0:T(8,128)(2,1)S(1)} %collective-permute-done.31.eu_p, ...), custom_call_target="tpu_custom_call" | custom-call | bytes 7602288 | tf_op jit(solution)/shard_map/pallas_call | solution.py:915
  213.6 10.6 %collective-permute-done.35.f_p.p1 = bf16[2,64,3712]{2,1,0:T(8,128)(2,1)S(1)} collective-permute-done((bf16[2,64,3712]{2,1,0:T(8,128)(2,1)}, bf16[2,64,3712]{2,1,0:T(8,128)(2,1)S(1)}, u32[]{:S(2)}, u32[]{:S(2)}) %collective-permute-start.35) | collective-permute-done | bytes 950304 | tf_op jit(solution)/shard_map/ppermute | solution.py:66
  231.2 5.8 %collective-permute-done.37.p2 = bf16[64,3712]{1,0:T(8,128)(2,1)S(1)} collective-permute-done((bf16[64,3712]{1,0:T(8,128)(2,1)}, bf16[64,3712]{1,0:T(8,128)(2,1)S(1)}, u32[]{:S(2)}, u32[]{:S(2)}) %collective-permute-start.37) | collective-permute-done | bytes 475168 | tf_op jit(solution)/shard_map/ppermute | solution.py:66
  238.5 3.2 %shard_map.278 = (bf16[16,7808]{1,0:T(8,128)(2,1)S(1)}, bf16[16,7808]{1,0:T(8,128)(2,1)S(1)}, bf16[16,7808]{1,0:T(8,128)(2,1)S(1)}, bf16[16,7808]{1,0:T(8,128)(2,1)S(1)}) custom-call(s32[7,4]{1,0:T(8,128)S(1)} %stack.185.places, bf16[2,64,3712]{2,1,0:T(8,128)(2,1)} %get-tuple-element.137.a_p.p0, bf16[2,64,3712]{2,1,0:T(8,128)(2,1)S(1)} %collective-permute-done.35.f_p.p1, ...), custom_call_target="tpu_custom_call" | custom-call | bytes 4751472 | tf_op jit(solution)/shard_map/pallas_call | solution.py:915
  241.8 2.9 %collective-permute-start.39 = (bf16[16,7808]{1,0:T(8,128)(2,1)S(1)}, bf16[16,7808]{1,0:T(8,128)(2,1)S(1)}, u32[]{:S(2)}, u32[]{:S(2)}) collective-permute-start(bf16[16,7808]{1,0:T(8,128)(2,1)S(1)} %get-tuple-element.144), channel_id=1, source_target_pairs={{0,1},{1,2},{2,3},{3,0},{4,5},{5,6},{6,7},{7,4},{8,9},{9,10},{10,1... | collective-permute-start | bytes 749576 | tf_op jit(solution)/shard_map/ppermute | solution.py:66
  244.7 3.5 %collective-permute-start.40 = (bf16[16,7808]{1,0:T(8,128)(2,1)S(1)}, bf16[16,7808]{1,0:T(8,128)(2,1)S(1)}, u32[]{:S(2)}, u32[]{:S(2)}) collective-permute-start(bf16[16,7808]{1,0:T(8,128)(2,1)S(1)} %get-tuple-element.145), channel_id=1, source_target_pairs={{0,2},{1,3},{2,0},{3,1},{4,6},{5,7},{6,4},{7,5},{8,10},{9,11},{10,... | collective-permute-start | bytes 749576 | tf_op jit(solution)/shard_map/ppermute | solution.py:66
  249.2 3.9 %collective-permute-done.39.o1 = bf16[16,7808]{1,0:T(8,128)(2,1)S(1)} collective-permute-done((bf16[16,7808]{1,0:T(8,128)(2,1)S(1)}, bf16[16,7808]{1,0:T(8,128)(2,1)S(1)}, u32[]{:S(2)}, u32[]{:S(2)}) %collective-permute-start.39) | collective-permute-done | bytes 249888 | tf_op jit(solution)/shard_map/ppermute | solution.py:66
  253.1 3.0 %collective-permute-done.40.o2 = bf16[16,7808]{1,0:T(8,128)(2,1)S(1)} collective-permute-done((bf16[16,7808]{1,0:T(8,128)(2,1)S(1)}, bf16[16,7808]{1,0:T(8,128)(2,1)S(1)}, u32[]{:S(2)}, u32[]{:S(2)}) %collective-permute-start.40) | collective-permute-done | bytes 249888 | tf_op jit(solution)/shard_map/ppermute | solution.py:66
  (174 shorter events, 79.8 us)
Async XLA Ops:
  5.7 16.8 %collective-permute-start = (bf16[256,1024]{1,0:T(8,128)(2,1)S(1)}, bf16[256,1024]{1,0:T(8,128)(2,1)S(1)}, u32[]{:S(2)}, u32[]{:S(2)}) collective-permute-start(bf16[256,1024]{1,0:T(8,128)(2,1)S(1)} %pad_maximum_fusion.1), channel_id=1, source_target_pairs={{0,32},{1,33},{2,34},{3,35},{4,36},{5,37},{6,38},{7,39},{8,40},{9,... | collective-permute-start | bytes 1572872 | tf_op jit(solution)/shard_map/ppermute | solution.py:66
  10.5 12.0 %collective-permute-start.4 = (bf16[16,7808]{1,0:T(8,128)(2,1)S(1)}, bf16[16,7808]{1,0:T(8,128)(2,1)S(1)}, u32[]{:S(2)}, u32[]{:S(2)}) collective-permute-start(bf16[16,7808]{1,0:T(8,128)(2,1)S(1)} %shard_map.264.p0), channel_id=1, source_target_pairs={{0,3},{1,0},{2,1},{3,2},{4,7},{5,4},{6,5},{7,6},{8,11},{9,8},{10,9... | collective-permute-start | bytes 749576 | tf_op jit(solution)/shard_map/ppermute | solution.py:66
  24.3 12.0 %collective-permute-start.6 = (bf16[2,32,3712]{2,1,0:T(8,128)(2,1)}, bf16[2,32,3712]{2,1,0:T(8,128)(2,1)S(1)}, u32[]{:S(2)}, u32[]{:S(2)}) collective-permute-start(bf16[2,32,3712]{2,1,0:T(8,128)(2,1)} %get-tuple-element.88.refs_0_), channel_id=1, source_target_pairs={{0,8},{1,9},{2,10},{3,11},{4,12},{5,13},{6,14},{7,15},{8,16},{9,17... | collective-permute-start | bytes 1425416 | tf_op jit(solution)/shard_map/ppermute | solution.py:66
  26.3 12.4 %collective-permute-start.8 = (bf16[2,32,3712]{2,1,0:T(8,128)(2,1)}, bf16[2,32,3712]{2,1,0:T(8,128)(2,1)S(1)}, u32[]{:S(2)}, u32[]{:S(2)}) collective-permute-start(bf16[2,32,3712]{2,1,0:T(8,128)(2,1)} %get-tuple-element.89.refs_3_), channel_id=1, source_target_pairs={{0,4},{1,5},{2,6},{3,7},{4,64},{5,65},{6,66},{7,67},{8,12},{9,13},... | collective-permute-start | bytes 1425416 | tf_op jit(solution)/shard_map/ppermute | solution.py:66
  27.8 13.1 %collective-permute-start.10 = (bf16[2,32,3712]{2,1,0:T(8,128)(2,1)}, bf16[2,32,3712]{2,1,0:T(8,128)(2,1)S(1)}, u32[]{:S(2)}, u32[]{:S(2)}) collective-permute-start(bf16[2,32,3712]{2,1,0:T(8,128)(2,1)} %get-tuple-element.88.refs_0_), channel_id=1, source_target_pairs={{0,24},{1,25},{2,26},{3,27},{4,28},{5,29},{6,30},{7,31},{8,0},{9,1... | collective-permute-start | bytes 1425416 | tf_op jit(solution)/shard_map/ppermute | solution.py:66
  30.0 11.0 %collective-permute-start.11 = (bf16[2,32,3712]{2,1,0:T(8,128)(2,1)}, bf16[2,32,3712]{2,1,0:T(8,128)(2,1)}, u32[]{:S(2)}, u32[]{:S(2)}) collective-permute-start(bf16[2,32,3712]{2,1,0:T(8,128)(2,1)} %get-tuple-element.89.refs_3_), channel_id=1, source_target_pairs={{0,68},{1,69},{2,70},{3,71},{4,0},{5,1},{6,2},{7,3},{8,76},{9,77},... | collective-permute-start | bytes 1425416 | tf_op jit(solution)/shard_map/ppermute | solution.py:66
  36.4 11.5 %collective-permute-start.7 = (bf16[2,32,3712]{2,1,0:T(8,128)(2,1)S(1)}, bf16[2,32,3712]{2,1,0:T(8,128)(2,1)S(1)}, u32[]{:S(2)}, u32[]{:S(2)}) collective-permute-start(bf16[2,32,3712]{2,1,0:T(8,128)(2,1)S(1)} %collective-permute-done.6.refs_1_), channel_id=1, source_target_pairs={{0,8},{1,9},{2,10},{3,11},{4,12},{5,13},{6,14},{7,15},{8,16},{9,17... | collective-permute-start | bytes 1425416 | tf_op jit(solution)/shard_map/ppermute | solution.py:66
  51.0 19.5 %collective-permute-start.13 = (bf16[2,4,32,1408]{3,2,1,0:T(8,128)(2,1)}, bf16[2,4,32,1408]{3,2,1,0:T(8,128)(2,1)}, u32[]{:S(2)}, u32[]{:S(2)}) collective-permute-start(bf16[2,4,32,1408]{3,2,1,0:T(8,128)(2,1)} %get-tuple-element.94.p0.wp0), channel_id=1, source_target_pairs={{0,68},{1,69},{2,70},{3,71},{4,0},{5,1},{6,2},{7,3},{8,76},{9,77},... | collective-permute-start | bytes 2162696 | tf_op jit(solution)/shard_map/ppermute | solution.py:66
  53.2 19.7 %collective-permute-start.12 = (bf16[2,4,32,1408]{3,2,1,0:T(8,128)(2,1)}, bf16[2,4,32,1408]{3,2,1,0:T(8,128)(2,1)}, u32[]{:S(2)}, u32[]{:S(2)}) collective-permute-start(bf16[2,4,32,1408]{3,2,1,0:T(8,128)(2,1)} %get-tuple-element.94.p0.wp0), channel_id=1, source_target_pairs={{0,4},{1,5},{2,6},{3,7},{4,64},{5,65},{6,66},{7,67},{8,12},{9,13},... | collective-permute-start | bytes 2162696 | tf_op jit(solution)/shard_map/ppermute | solution.py:66
  53.2 20.4 %collective-permute-start.15 = (bf16[2,2,2,32,1408]{4,3,2,1,0:T(8,128)(2,1)}, bf16[2,2,2,32,1408]{4,3,2,1,0:T(8,128)(2,1)}, u32[]{:S(2)}, u32[]{:S(2)}) collective-permute-start(bf16[2,2,2,32,1408]{4,3,2,1,0:T(8,128)(2,1)} %get-tuple-element.95.q0.wq0), channel_id=1, source_target_pairs={{0,8},{1,9},{2,10},{3,11},{4,12},{5,13},{6,14},{7,15},{8,16},{9,17... | collective-permute-start | bytes 2162696 | tf_op jit(solution)/shard_map/ppermute | solution.py:66
  56.9 36.1 %collective-permute-start.19 = (bf16[2,4,32,2304]{3,2,1,0:T(8,128)(2,1)}, bf16[2,4,32,2304]{3,2,1,0:T(8,128)(2,1)S(1)}, u32[]{:S(2)}, u32[]{:S(2)}) collective-permute-start(bf16[2,4,32,2304]{3,2,1,0:T(8,128)(2,1)} %get-tuple-element.100.p0), channel_id=1, source_target_pairs={{0,4},{1,5},{2,6},{3,7},{4,64},{5,65},{6,66},{7,67},{8,12},{9,13},... | collective-permute-start | bytes 3538952 | tf_op jit(solution)/shard_map/ppermute | solution.py:66
  57.0 38.4 %collective-permute-start.22 = (bf16[2,2,2,32,2304]{4,3,2,1,0:T(8,128)(2,1)}, bf16[2,2,2,32,2304]{4,3,2,1,0:T(8,128)(2,1)}, u32[]{:S(2)}, u32[]{:S(2)}) collective-permute-start(bf16[2,2,2,32,2304]{4,3,2,1,0:T(8,128)(2,1)} %get-tuple-element.101.q0), channel_id=1, source_target_pairs={{0,8},{1,9},{2,10},{3,11},{4,12},{5,13},{6,14},{7,15},{8,16},{9,17... | collective-permute-start | bytes 3538952 | tf_op jit(solution)/shard_map/ppermute | solution.py:66
  70.4 21.0 %collective-permute-start.16 = (bf16[2,2,2,32,1408]{4,3,2,1,0:T(8,128)(2,1)}, bf16[2,2,2,32,1408]{4,3,2,1,0:T(8,128)(2,1)S(1)}, u32[]{:S(2)}, u32[]{:S(2)}) collective-permute-start(bf16[2,2,2,32,1408]{4,3,2,1,0:T(8,128)(2,1)} %get-tuple-element.95.q0.wq0), channel_id=1, source_target_pairs={{0,24},{1,25},{2,26},{3,27},{4,28},{5,29},{6,30},{7,31},{8,0},{9,1... | collective-permute-start | bytes 2162696 | tf_op jit(solution)/shard_map/ppermute | solution.py:66
  72.9 22.5 %collective-permute-start.14 = (bf16[2,4,32,1408]{3,2,1,0:T(8,128)(2,1)}, bf16[2,4,32,1408]{3,2,1,0:T(8,128)(2,1)S(1)}, u32[]{:S(2)}, u32[]{:S(2)}) collective-permute-start(bf16[2,4,32,1408]{3,2,1,0:T(8,128)(2,1)} %collective-permute-done.12.p1.wp1), channel_id=1, source_target_pairs={{0,4},{1,5},{2,6},{3,7},{4,64},{5,65},{6,66},{7,67},{8,12},{9,13},... | collective-permute-start | bytes 2162696 | tf_op jit(solution)/shard_map/ppermute | solution.py:66
  73.6 27.1 %collective-permute-start.17 = (bf16[2,2,2,32,1408]{4,3,2,1,0:T(8,128)(2,1)}, bf16[2,2,2,32,1408]{4,3,2,1,0:T(8,128)(2,1)S(1)}, u32[]{:S(2)}, u32[]{:S(2)}) collective-permute-start(bf16[2,2,2,32,1408]{4,3,2,1,0:T(8,128)(2,1)} %collective-permute-done.15.q1.wq1), channel_id=1, source_target_pairs={{0,8},{1,9},{2,10},{3,11},{4,12},{5,13},{6,14},{7,15},{8,16},{9,17... | collective-permute-start | bytes 2162696 | tf_op jit(solution)/shard_map/ppermute | solution.py:66
  91.5 24.2 %collective-permute-start.20 = (bf16[2,4,32,2304]{3,2,1,0:T(8,128)(2,1)S(1)}, bf16[2,4,32,2304]{3,2,1,0:T(8,128)(2,1)S(1)}, u32[]{:S(2)}, u32[]{:S(2)}) collective-permute-start(bf16[2,4,32,2304]{3,2,1,0:T(8,128)(2,1)S(1)} %copy-done), channel_id=1, source_target_pairs={{0,68},{1,69},{2,70},{3,71},{4,0},{5,1},{6,2},{7,3},{8,76},{9,77},... | collective-permute-start | bytes 3538952 | tf_op jit(solution)/shard_map/ppermute | solution.py:66
  93.0 25.6 %collective-permute-start.23 = (bf16[2,2,2,32,2304]{4,3,2,1,0:T(8,128)(2,1)}, bf16[2,2,2,32,2304]{4,3,2,1,0:T(8,128)(2,1)S(1)}, u32[]{:S(2)}, u32[]{:S(2)}) collective-permute-start(bf16[2,2,2,32,2304]{4,3,2,1,0:T(8,128)(2,1)} %get-tuple-element.101.q0), channel_id=1, source_target_pairs={{0,24},{1,25},{2,26},{3,27},{4,28},{5,29},{6,30},{7,31},{8,0},{9,1... | collective-permute-start | bytes 3538952 | tf_op jit(solution)/shard_map/ppermute | solution.py:66
  95.3 23.2 %collective-permute-start.21 = (bf16[2,4,32,2304]{3,2,1,0:T(8,128)(2,1)S(1)}, bf16[2,4,32,2304]{3,2,1,0:T(8,128)(2,1)S(1)}, u32[]{:S(2)}, u32[]{:S(2)}) collective-permute-start(bf16[2,4,32,2304]{3,2,1,0:T(8,128)(2,1)S(1)} %collective-permute-done.19.p1), channel_id=1, source_target_pairs={{0,4},{1,5},{2,6},{3,7},{4,64},{5,65},{6,66},{7,67},{8,12},{9,13},... | collective-permute-start | bytes 3538952 | tf_op jit(solution)/shard_map/ppermute | solution.py:66
  95.5 23.9 %collective-permute-start.24 = (bf16[2,2,2,32,2304]{4,3,2,1,0:T(8,128)(2,1)}, bf16[2,2,2,32,2304]{4,3,2,1,0:T(8,128)(2,1)S(1)}, u32[]{:S(2)}, u32[]{:S(2)}) collective-permute-start(bf16[2,2,2,32,2304]{4,3,2,1,0:T(8,128)(2,1)} %collective-permute-done.22.q1), channel_id=1, source_target_pairs={{0,8},{1,9},{2,10},{3,11},{4,12},{5,13},{6,14},{7,15},{8,16},{9,17... | collective-permute-start | bytes 3538952 | tf_op jit(solution)/shard_map/ppermute | solution.py:66
  135.2 29.1 %collective-permute-start.28 = (bf16[2,4,64,2304]{3,2,1,0:T(8,128)(2,1)}, bf16[2,4,64,2304]{3,2,1,0:T(8,128)(2,1)S(1)}, u32[]{:S(2)}, u32[]{:S(2)}) collective-permute-start(bf16[2,4,64,2304]{3,2,1,0:T(8,128)(2,1)} %get-tuple-element.124), channel_id=1, source_target_pairs={{0,4},{1,5},{2,6},{3,7},{4,0},{5,1},{6,2},{7,3},{8,12},{9,13},{10,... | collective-permute-start | bytes 7077896 | tf_op jit(solution)/shard_map/ppermute | solution.py:66
  136.3 29.1 %collective-permute-start.30 = (bf16[2,4,64,2304]{3,2,1,0:T(8,128)(2,1)}, bf16[2,4,64,2304]{3,2,1,0:T(8,128)(2,1)S(1)}, u32[]{:S(2)}, u32[]{:S(2)}) collective-permute-start(bf16[2,4,64,2304]{3,2,1,0:T(8,128)(2,1)} %get-tuple-element.128), channel_id=1, source_target_pairs={{0,8},{1,9},{2,10},{3,11},{4,12},{5,13},{6,14},{7,15},{8,0},{9,1},... | collective-permute-start | bytes 7077896 | tf_op jit(solution)/shard_map/ppermute | solution.py:66
  153.9 29.8 %collective-permute-start.27 = (bf16[2,4,64,1408]{3,2,1,0:T(8,128)(2,1)}, bf16[2,4,64,1408]{3,2,1,0:T(8,128)(2,1)S(1)}, u32[]{:S(2)}, u32[]{:S(2)}) collective-permute-start(bf16[2,4,64,1408]{3,2,1,0:T(8,128)(2,1)} %get-tuple-element.120), channel_id=1, source_target_pairs={{0,4},{1,5},{2,6},{3,7},{4,0},{5,1},{6,2},{7,3},{8,12},{9,13},{10,... | collective-permute-start | bytes 4325384 | tf_op jit(solution)/shard_map/ppermute | solution.py:66
  155.7 30.6 %collective-permute-start.29 = (bf16[2,4,64,1408]{3,2,1,0:T(8,128)(2,1)}, bf16[2,4,64,1408]{3,2,1,0:T(8,128)(2,1)S(1)}, u32[]{:S(2)}, u32[]{:S(2)}) collective-permute-start(bf16[2,4,64,1408]{3,2,1,0:T(8,128)(2,1)} %get-tuple-element.126), channel_id=1, source_target_pairs={{0,8},{1,9},{2,10},{3,11},{4,12},{5,13},{6,14},{7,15},{8,0},{9,1},... | collective-permute-start | bytes 4325384 | tf_op jit(solution)/shard_map/ppermute | solution.py:66
  170.4 29.1 %collective-permute-start.32 = (bf16[4,64,2304]{2,1,0:T(8,128)(2,1)}, bf16[4,64,2304]{2,1,0:T(8,128)(2,1)S(1)}, u32[]{:S(2)}, u32[]{:S(2)}) collective-permute-start(bf16[4,64,2304]{2,1,0:T(8,128)(2,1)} %get-tuple-element.132), channel_id=1, source_target_pairs={{0,68},{1,69},{2,70},{3,71},{4,64},{5,65},{6,66},{7,67},{8,76},{9,... | collective-permute-start | bytes 3538952 | tf_op jit(solution)/shard_map/ppermute | solution.py:66
  173.4 26.1 %collective-permute-start.34 = (bf16[4,64,2304]{2,1,0:T(8,128)(2,1)}, bf16[4,64,2304]{2,1,0:T(8,128)(2,1)}, u32[]{:S(2)}, u32[]{:S(2)}) collective-permute-start(bf16[4,64,2304]{2,1,0:T(8,128)(2,1)} %get-tuple-element.136), channel_id=1, source_target_pairs={{0,24},{1,25},{2,26},{3,27},{4,28},{5,29},{6,30},{7,31},{8,16},{9,... | collective-permute-start | bytes 3538952 | tf_op jit(solution)/shard_map/ppermute | solution.py:66
  190.3 12.9 %collective-permute-start.31 = (bf16[4,64,1408]{2,1,0:T(8,128)(2,1)}, bf16[4,64,1408]{2,1,0:T(8,128)(2,1)S(1)}, u32[]{:S(2)}, u32[]{:S(2)}) collective-permute-start(bf16[4,64,1408]{2,1,0:T(8,128)(2,1)} %get-tuple-element.130), channel_id=1, source_target_pairs={{0,68},{1,69},{2,70},{3,71},{4,64},{5,65},{6,66},{7,67},{8,76},{9,... | collective-permute-start | bytes 2162696 | tf_op jit(solution)/shard_map/ppermute | solution.py:66
  193.7 12.8 %collective-permute-start.33 = (bf16[4,64,1408]{2,1,0:T(8,128)(2,1)}, bf16[4,64,1408]{2,1,0:T(8,128)(2,1)}, u32[]{:S(2)}, u32[]{:S(2)}) collective-permute-start(bf16[4,64,1408]{2,1,0:T(8,128)(2,1)} %get-tuple-element.134), channel_id=1, source_target_pairs={{0,24},{1,25},{2,26},{3,27},{4,28},{5,29},{6,30},{7,31},{8,16},{9,... | collective-permute-start | bytes 2162696 | tf_op jit(solution)/shard_map/ppermute | solution.py:66
  210.1 14.0 %collective-permute-start.35 = (bf16[2,64,3712]{2,1,0:T(8,128)(2,1)}, bf16[2,64,3712]{2,1,0:T(8,128)(2,1)S(1)}, u32[]{:S(2)}, u32[]{:S(2)}) collective-permute-start(bf16[2,64,3712]{2,1,0:T(8,128)(2,1)} %get-tuple-element.138), channel_id=1, source_target_pairs={{0,8},{1,9},{2,10},{3,11},{4,12},{5,13},{6,14},{7,15},{8,0},{9,1},... | collective-permute-start | bytes 2850824 | tf_op jit(solution)/shard_map/ppermute | solution.py:66
  210.2 14.0 %collective-permute-start.36 = (bf16[2,64,3712]{2,1,0:T(8,128)(2,1)}, bf16[2,64,3712]{2,1,0:T(8,128)(2,1)S(1)}, u32[]{:S(2)}, u32[]{:S(2)}) collective-permute-start(bf16[2,64,3712]{2,1,0:T(8,128)(2,1)} %get-tuple-element.140), channel_id=1, source_target_pairs={{0,4},{1,5},{2,6},{3,7},{4,0},{5,1},{6,2},{7,3},{8,12},{9,13},{10,... | collective-permute-start | bytes 2850824 | tf_op jit(solution)/shard_map/ppermute | solution.py:66
  213.0 18.0 %collective-permute-start.26 = (f32[128,1024]{1,0:T(8,128)}, f32[128,1024]{1,0:T(8,128)S(1)}, u32[]{:S(2)}, u32[]{:S(2)}) collective-permute-start(f32[128,1024]{1,0:T(8,128)} %get-tuple-element.117), channel_id=1, source_target_pairs={{0,32},{1,33},{2,34},{3,35},{4,36},{5,37},{6,38},{7,39},{8,40},{9,... | collective-permute-start | bytes 1572872 | tf_op jit(solution)/shard_map/ppermute | solution.py:66
  241.8 11.3 %collective-permute-start.39 = (bf16[16,7808]{1,0:T(8,128)(2,1)S(1)}, bf16[16,7808]{1,0:T(8,128)(2,1)S(1)}, u32[]{:S(2)}, u32[]{:S(2)}) collective-permute-start(bf16[16,7808]{1,0:T(8,128)(2,1)S(1)} %get-tuple-element.144), channel_id=1, source_target_pairs={{0,1},{1,2},{2,3},{3,0},{4,5},{5,6},{6,7},{7,4},{8,9},{9,10},{10,1... | collective-permute-start | bytes 749576 | tf_op jit(solution)/shard_map/ppermute | solution.py:66
  244.7 11.4 %collective-permute-start.40 = (bf16[16,7808]{1,0:T(8,128)(2,1)S(1)}, bf16[16,7808]{1,0:T(8,128)(2,1)S(1)}, u32[]{:S(2)}, u32[]{:S(2)}) collective-permute-start(bf16[16,7808]{1,0:T(8,128)(2,1)S(1)} %get-tuple-element.145), channel_id=1, source_target_pairs={{0,2},{1,3},{2,0},{3,1},{4,6},{5,7},{6,4},{7,5},{8,10},{9,11},{10,... | collective-permute-start | bytes 749576 | tf_op jit(solution)/shard_map/ppermute | solution.py:66
  (34 other events, 255.8 us)
where the time goes:
time: 264 us; the launch traced here: 262 us
  waiting for transfers between devices  113 us (43%)
  Pallas kernels  73.2 us (28%)
  starting transfers between devices  59 us (22%)
  local copies, waits for them, and re-layouts  8.34 us (3%)
  other arithmetic  7.07 us (3%)
    ppermute x43, waiting for transfers between devices, send(): return lax.ppermute(value, AXES, route)  113 us
    pallas_call x18, Pallas kernels, kernel(): pl.pallas_call(body, out_shape=[HB(s, d) if at is HB else jax.ShapeDtypeS...  73.2 us
    ppermute x43, starting transfers between devices, send(): return lax.ppermute(value, AXES, route)  59 us
  transfers between devices with their start and end apart: 43, of which 26 were waited for; matrix products, arithmetic and copies ran while one was open for 3% of the time, Pallas kernels for 19%

commit v1 on v0

--- a/solution.py
+++ b/solution.py
@@ -591,12 +591,17 @@
 
     put(bp, True, 0, FC)
     emit_columns(saves, bp, places, 0, (p0, p1), FC, PI)
+    q_copies = [(bq.at[places[6, j]], (q0, q1)[j // 2].at[j % 2]) for j in range(4)]
 
     @pl.loop(0, 3)
     def _(part):
         put(bq, False, 768 * (part + 1), 768 * part)
-
-    emit_columns(saves, bq, places, 2, (q0, q1), 0, LATE)
+        columns = pl.ds(pl.multiple_of(768 * part, 256), 768)
+        for j, (source, target) in enumerate(q_copies):
+            pltpu.make_async_copy(source.at[:, :, columns], target.at[:, :, columns], out_sems.at[8 + j]).start()
+
+    for j, (source, target) in enumerate(q_copies):
+        pltpu.make_async_copy(source, target, out_sems.at[8 + j]).wait()
     saves.wait()
 
 

time: 264 us -> 263 us (level)
  transfers between devices with their start and end apart: 43 -> 43, of which waited for: 26 -> 26; matrix products, arithmetic and copies ran while one was open for 3% -> 3% of each run, Pallas kernels for 19% -> 18%
where the time goes in v1:
time: 263 us; the launch traced here: 261 us
  waiting for transfers between devices  113 us (43%)
  Pallas kernels  72.3 us (27%)
  starting transfers between devices  59 us (22%)
  local copies, waits for them, and re-layouts  8.34 us (3%)
  other arithmetic  7.07 us (3%)
    ppermute x43, waiting for transfers between devices, send(): return lax.ppermute(value, AXES, route)  113 us
    pallas_call x18, Pallas kernels, kernel(): pl.pallas_call(body, out_shape=[HB(s, d) if at is HB else jax.ShapeDtypeS...  72.3 us
    ppermute x43, starting transfers between devices, send(): return lax.ppermute(value, AXES, route)  59 us
  transfers between devices with their start and end apart: 43, of which 26 were waited for; matrix products, arithmetic and copies ran while one was open for 3% of the time, Pallas kernels for 18%

profile of v1, /device:TPU:0, one launch (start us, length us, event | category | flops | bytes accessed | tf_op | source)
XLA Modules:
  0.0 261.3 jit_solution(7311108996736566932)
XLA Ops:
  7.1 3.4 %collective-permute-start.5 = (bf16[16,7808]{1,0:T(8,128)(2,1)S(1)}, bf16[16,7808]{1,0:T(8,128)(2,1)S(1)}, u32[]{:S(2)}, u32[]{:S(2)}) collective-permute-start(bf16[16,7808]{1,0:T(8,128)(2,1)S(1)} %shard_map.264.p0), channel_id=1, source_target_pairs={{0,2},{1,3},{2,0},{3,1},{4,6},{5,7},{6,4},{7,5},{8,10},{9,11},{10,... | collective-permute-start | bytes 749576 | tf_op jit(solution)/shard_map/ppermute | solution.py:66
  13.9 3.7 %collective-permute-done.5.p3 = bf16[16,7808]{1,0:T(8,128)(2,1)S(1)} collective-permute-done((bf16[16,7808]{1,0:T(8,128)(2,1)S(1)}, bf16[16,7808]{1,0:T(8,128)(2,1)S(1)}, u32[]{:S(2)}, u32[]{:S(2)}) %collective-permute-start.5) | collective-permute-done | bytes 249888 | tf_op jit(solution)/shard_map/ppermute | solution.py:66
  17.6 4.9 %collective-permute-done.4.p2 = bf16[16,7808]{1,0:T(8,128)(2,1)S(1)} collective-permute-done((bf16[16,7808]{1,0:T(8,128)(2,1)S(1)}, bf16[16,7808]{1,0:T(8,128)(2,1)S(1)}, u32[]{:S(2)}, u32[]{:S(2)}) %collective-permute-start.4) | collective-permute-done | bytes 249888 | tf_op jit(solution)/shard_map/ppermute | solution.py:66
  31.7 4.6 %collective-permute-done.6.refs_1_ = bf16[2,32,3712]{2,1,0:T(8,128)(2,1)S(1)} collective-permute-done((bf16[2,32,3712]{2,1,0:T(8,128)(2,1)}, bf16[2,32,3712]{2,1,0:T(8,128)(2,1)S(1)}, u32[]{:S(2)}, u32[]{:S(2)}) %collective-permute-start.6) | collective-permute-done | bytes 475168 | tf_op jit(solution)/shard_map/ppermute | solution.py:66
  41.7 3.4 %shard_map.266 = (bf16[2,4,32,1408]{3,2,1,0:T(8,128)(2,1)}, bf16[2,2,2,32,1408]{4,3,2,1,0:T(8,128)(2,1)}, bf16[2,4,32,2304]{3,2,1,0:T(8,128)(2,1)}, bf16[2,2,2,32,2304]{4,3,2,1,0:T(8,128)(2,1)}) custom-call(s32[7,4]{1,0:T(8,128)S(1)} %stack.185.places, bf16[2,32,3712]{2,1,0:T(8,128)(2,1)} %get-tuple-element.88.refs_0_, bf16[2,32,3712]{2,1,0:T(8,128)(2,1)} %copy-done.16, ...), custom_call_target="tpu_custom_call" | custom-call | bytes 2850928 | tf_op jit(solution)/shard_map/pallas_call | solution.py:920
  45.1 2.8 %collective-permute-done.7.refs_0_ = bf16[2,32,3712]{2,1,0:T(8,128)(2,1)S(1)} collective-permute-done((bf16[2,32,3712]{2,1,0:T(8,128)(2,1)S(1)}, bf16[2,32,3712]{2,1,0:T(8,128)(2,1)S(1)}, u32[]{:S(2)}, u32[]{:S(2)}) %collective-permute-start.7) | collective-permute-done | bytes 475168 | tf_op jit(solution)/shard_map/ppermute | solution.py:66
  53.2 3.6 %collective-permute-start.15 = (bf16[2,2,2,32,1408]{4,3,2,1,0:T(8,128)(2,1)}, bf16[2,2,2,32,1408]{4,3,2,1,0:T(8,128)(2,1)}, u32[]{:S(2)}, u32[]{:S(2)}) collective-permute-start(bf16[2,2,2,32,1408]{4,3,2,1,0:T(8,128)(2,1)} %get-tuple-element.95.q0.wq0), channel_id=1, source_target_pairs={{0,8},{1,9},{2,10},{3,11},{4,12},{5,13},{6,14},{7,15},{8,16},{9,17... | collective-permute-start | bytes 2162696 | tf_op jit(solution)/shard_map/ppermute | solution.py:66
  59.0 11.4 %collective-permute-done.13.p2.wp2 = bf16[2,4,32,1408]{3,2,1,0:T(8,128)(2,1)} collective-permute-done((bf16[2,4,32,1408]{3,2,1,0:T(8,128)(2,1)}, bf16[2,4,32,1408]{3,2,1,0:T(8,128)(2,1)}, u32[]{:S(2)}, u32[]{:S(2)}) %collective-permute-start.13) | collective-permute-done | bytes 720928 | tf_op jit(solution)/shard_map/ppermute | solution.py:66
  74.4 17.0 %collective-permute-done.16.q2.wq2 = bf16[2,2,2,32,1408]{4,3,2,1,0:T(8,128)(2,1)S(1)} collective-permute-done((bf16[2,2,2,32,1408]{4,3,2,1,0:T(8,128)(2,1)}, bf16[2,2,2,32,1408]{4,3,2,1,0:T(8,128)(2,1)S(1)}, u32[]{:S(2)}, u32[]{:S(2)}) %collective-permute-start.16) | collective-permute-done | bytes 720928 | tf_op jit(solution)/shard_map/ppermute | solution.py:66
  95.6 5.1 %collective-permute-done.17.q3.wq3 = bf16[2,2,2,32,1408]{4,3,2,1,0:T(8,128)(2,1)S(1)} collective-permute-done((bf16[2,2,2,32,1408]{4,3,2,1,0:T(8,128)(2,1)}, bf16[2,2,2,32,1408]{4,3,2,1,0:T(8,128)(2,1)S(1)}, u32[]{:S(2)}, u32[]{:S(2)}) %collective-permute-start.17) | collective-permute-done | bytes 720928 | tf_op jit(solution)/shard_map/ppermute | solution.py:66
  101.6 8.6 %shard_map.268 = (f32[264,1024]{1,0:T(8,128)S(1)}, f32[4,768]{1,0:T(4,128)S(1)}, f32[8,1024]{1,0:T(8,128)S(1)}, f32[8,768]{1,0:T(8,128)S(1)}, bf16[256,1024]{1,0...) custom-call(s32[7,4]{1,0:T(8,128)S(1)} %stack.185.places, ...), custom_call_target="tpu_custom_call" | custom-call | flops 1509949440 | bytes 6971504 | tf_op jit(solution)/shard_map/pallas_call | solution.py:920
  115.7 2.9 %collective-permute-done.23.q2 = bf16[2,2,2,32,2304]{4,3,2,1,0:T(8,128)(2,1)S(1)} collective-permute-done((bf16[2,2,2,32,2304]{4,3,2,1,0:T(8,128)(2,1)}, bf16[2,2,2,32,2304]{4,3,2,1,0:T(8,128)(2,1)S(1)}, u32[]{:S(2)}, u32[]{:S(2)}) %collective-permute-start.23) | collective-permute-done | bytes 1179680 | tf_op jit(solution)/shard_map/ppermute | solution.py:66
  119.3 9.2 %shard_map.270 = (bf16[256,1536]{1,0:T(8,128)(2,1)S(1)}, bf16[256,3072]{1,0:T(8,128)(2,1)S(1)}, f32[128,1024]{1,0:T(8,128)}, f32[384,1024]{1,0:T(8,128)}) custom-call(s32[7,4]{1,0:T(8,128)S(1)} %stack.185.places, bf16[256,1024]{1,0:T(8,128)(2,1)S(1)} %pad_maximum_fusion.2.cot, bf16[256,1024]{1,0:T(8,128)(2,1)S(1)} %get-tuple-element.98.normed2, ...), custom_call_target="tpu_custom_call" | custom-call | flops 4831838208 | bytes 11010160 | tf_op jit(solution)/shard_map/pallas_call | solution.py:920
  128.6 5.7 %shard_map.272 = (bf16[2,4,64,2304]{3,2,1,0:T(8,128)(2,1)}, bf16[2,4,64,2304]{3,2,1,0:T(8,128)(2,1)}, bf16[2,4,64,2304]{3,2,1,0:T(8,128)(2,1)}, bf16[2,4,64,2304]{3,2,1,0:T(8,128)(2,1)}) custom-call(s32[7,4]{1,0:T(8,128)S(1)} %stack.185.places, bf16[256,1024]{1,0:T(8,128)(2,1)S(1)} %pad_maximum_fusion.2.cot, ...), custom_call_target="tpu_custom_call" | custom-call | flops 2415919104 | bytes 3407984 | tf_op jit(solution)/shard_map/pallas_call | solution.py:920
  137.1 15.9 %shard_map.271 = (f32[128,1024]{1,0:T(8,128)}, f32[128,1024]{1,0:T(8,128)}, f32[128,1024]{1,0:T(8,128)}, bf16[2,4,64,1408]{3,2,1,0:T(8,128)(2,1)}, bf16[2,4,64,1...) custom-call(s32[7,4]{1,0:T(8,128)S(1)} %stack.185.places, ...), custom_call_target="tpu_custom_call" | custom-call | flops 2415919104 | bytes 18243696 | tf_op jit(solution)/shard_map/pallas_call | solution.py:920
  154.8 8.6 %collective-permute-done.28.d_p.f_p = bf16[2,4,64,2304]{3,2,1,0:T(8,128)(2,1)S(1)} collective-permute-done((bf16[2,4,64,2304]{3,2,1,0:T(8,128)(2,1)}, bf16[2,4,64,2304]{3,2,1,0:T(8,128)(2,1)S(1)}, u32[]{:S(2)}, u32[]{:S(2)}) %collective-permute-start.28) | collective-permute-done | bytes 2359328 | tf_op jit(solution)/shard_map/ppermute | solution.py:66
  165.9 3.7 %shard_map.275 = (bf16[4,64,2304]{2,1,0:T(8,128)(2,1)}, bf16[4,64,2304]{2,1,0:T(8,128)(2,1)}) custom-call(bf16[2,4,64,2304]{3,2,1,0:T(8,128)(2,1)} %get-tuple-element.123.c_p.a_p, bf16[2,4,64,2304]{3,2,1,0:T(8,128)(2,1)} %copy-done.3, bf16[2,4,64,2304]{3,2,1,0:T(8,128)(2,1)} %get-tuple-element.127.c_q.a_q, bf16[2,4,64,2304]{3,2,1,0:T(8,128)(2,1)} %copy-done.4, ...), custom_call_target="tpu_custom_call" | custom-call | bytes 10878976 | tf_op jit(solution)/shard_map/pallas_call | solution.py:920
  169.6 3.0 %collective-permute-start.32 = (bf16[4,64,2304]{2,1,0:T(8,128)(2,1)}, bf16[4,64,2304]{2,1,0:T(8,128)(2,1)S(1)}, u32[]{:S(2)}, u32[]{:S(2)}) collective-permute-start(bf16[4,64,2304]{2,1,0:T(8,128)(2,1)} %get-tuple-element.132), channel_id=1, source_target_pairs={{0,68},{1,69},{2,70},{3,71},{4,64},{5,65},{6,66},{7,67},{8,76},{9,... | collective-permute-start | bytes 3538952 | tf_op jit(solution)/shard_map/ppermute | solution.py:66
  173.8 9.0 %collective-permute-done.27.b_p.f_p = bf16[2,4,64,1408]{3,2,1,0:T(8,128)(2,1)S(1)} collective-permute-done((bf16[2,4,64,1408]{3,2,1,0:T(8,128)(2,1)}, bf16[2,4,64,1408]{3,2,1,0:T(8,128)(2,1)S(1)}, u32[]{:S(2)}, u32[]{:S(2)}) %collective-permute-start.27) | collective-permute-done | bytes 1441824 | tf_op jit(solution)/shard_map/ppermute | solution.py:66
  186.6 2.8 %shard_map.274 = (bf16[4,64,1408]{2,1,0:T(8,128)(2,1)}, bf16[4,64,1408]{2,1,0:T(8,128)(2,1)}) custom-call(bf16[2,4,64,1408]{3,2,1,0:T(8,128)(2,1)} %get-tuple-element.119.a_p.rest_0_, bf16[2,4,64,1408]{3,2,1,0:T(8,128)(2,1)} %copy-done.7, bf16[2,4,64,1408]{3,2,1,0:T(8,128)(2,1)} %get-tuple-element.125.a_q, bf16[2,4,64,1408]{3,2,1,0:T(8,128)(2,1)} %copy-done.8), custom_call_target="tpu_custom_call" | custom-call | bytes 5767168 | tf_op jit(solution)/shard_map/pallas_call | solution.py:920
  189.5 3.4 %collective-permute-start.31 = (bf16[4,64,1408]{2,1,0:T(8,128)(2,1)}, bf16[4,64,1408]{2,1,0:T(8,128)(2,1)S(1)}, u32[]{:S(2)}, u32[]{:S(2)}) collective-permute-start(bf16[4,64,1408]{2,1,0:T(8,128)(2,1)} %get-tuple-element.130), channel_id=1, source_target_pairs={{0,68},{1,69},{2,70},{3,71},{4,64},{5,65},{6,66},{7,67},{8,76},{9,... | collective-permute-start | bytes 2162696 | tf_op jit(solution)/shard_map/ppermute | solution.py:66
  195.1 3.5 %shard_map.273 = (bf16[4,64,1408]{2,1,0:T(8,128)(2,1)S(1)}, bf16[4,64,2304]{2,1,0:T(8,128)(2,1)S(1)}, bf16[4,64,1408]{2,1,0:T(8,128)(2,1)S(1)}, bf16[4,64,2304]{2,1,0:T(8,128)(2,1)S(1)}) custom-call(bf16[2,4,64,1408]{3,2,1,0:T(8,128)(2,1)} %get-tuple-element.119.a_p.rest_0_, bf16[2,4,64,1408]{3,2,1,0:T(8,128)(2,1)} %copy-done.7, ...), custom_call_target="tpu_custom_call" | custom-call | bytes 15204352 | tf_op jit(solution)/shard_map/pallas_call | solution.py:920
  198.7 3.6 %collective-permute-done.31.eu_p = bf16[4,64,1408]{2,1,0:T(8,128)(2,1)S(1)} collective-permute-done((bf16[4,64,1408]{2,1,0:T(8,128)(2,1)}, bf16[4,64,1408]{2,1,0:T(8,128)(2,1)S(1)}, u32[]{:S(2)}, u32[]{:S(2)}) %collective-permute-start.31) | collective-permute-done | bytes 720928 | tf_op jit(solution)/shard_map/ppermute | solution.py:66
  202.3 3.3 %collective-permute-done.33.eu_q = bf16[4,64,1408]{2,1,0:T(8,128)(2,1)} collective-permute-done((bf16[4,64,1408]{2,1,0:T(8,128)(2,1)}, bf16[4,64,1408]{2,1,0:T(8,128)(2,1)}, u32[]{:S(2)}, u32[]{:S(2)}) %collective-permute-start.33) | collective-permute-done | bytes 720928 | tf_op jit(solution)/shard_map/ppermute | solution.py:66
  205.7 3.6 %shard_map.276 = (bf16[2,64,3712]{2,1,0:T(8,128)(2,1)}, bf16[2,64,3712]{2,1,0:T(8,128)(2,1)}, bf16[2,64,3712]{2,1,0:T(8,128)(2,1)}, bf16[2,64,3712]{2,1,0:T(8,128)(2,1)}) custom-call(s32[7,4]{1,0:T(8,128)S(1)} %stack.185.places, bf16[4,64,1408]{2,1,0:T(8,128)(2,1)S(1)} %get-tuple-element.129.eo_p, bf16[4,64,1408]{2,1,0:T(8,128)(2,1)S(1)} %collective-permute-done.31.eu_p, ...), custom_call_target="tpu_custom_call" | custom-call | bytes 7602288 | tf_op jit(solution)/shard_map/pallas_call | solution.py:920
  212.7 10.6 %collective-permute-done.35.f_p.p1 = bf16[2,64,3712]{2,1,0:T(8,128)(2,1)S(1)} collective-permute-done((bf16[2,64,3712]{2,1,0:T(8,128)(2,1)}, bf16[2,64,3712]{2,1,0:T(8,128)(2,1)S(1)}, u32[]{:S(2)}, u32[]{:S(2)}) %collective-permute-start.35) | collective-permute-done | bytes 950304 | tf_op jit(solution)/shard_map/ppermute | solution.py:66
  230.3 5.8 %collective-permute-done.37.p2 = bf16[64,3712]{1,0:T(8,128)(2,1)S(1)} collective-permute-done((bf16[64,3712]{1,0:T(8,128)(2,1)}, bf16[64,3712]{1,0:T(8,128)(2,1)S(1)}, u32[]{:S(2)}, u32[]{:S(2)}) %collective-permute-start.37) | collective-permute-done | bytes 475168 | tf_op jit(solution)/shard_map/ppermute | solution.py:66
  237.6 3.2 %shard_map.278 = (bf16[16,7808]{1,0:T(8,128)(2,1)S(1)}, bf16[16,7808]{1,0:T(8,128)(2,1)S(1)}, bf16[16,7808]{1,0:T(8,128)(2,1)S(1)}, bf16[16,7808]{1,0:T(8,128)(2,1)S(1)}) custom-call(s32[7,4]{1,0:T(8,128)S(1)} %stack.185.places, bf16[2,64,3712]{2,1,0:T(8,128)(2,1)} %get-tuple-element.137.a_p.p0, bf16[2,64,3712]{2,1,0:T(8,128)(2,1)S(1)} %collective-permute-done.35.f_p.p1, ...), custom_call_target="tpu_custom_call" | custom-call | bytes 4751472 | tf_op jit(solution)/shard_map/pallas_call | solution.py:920
  240.9 2.9 %collective-permute-start.39 = (bf16[16,7808]{1,0:T(8,128)(2,1)S(1)}, bf16[16,7808]{1,0:T(8,128)(2,1)S(1)}, u32[]{:S(2)}, u32[]{:S(2)}) collective-permute-start(bf16[16,7808]{1,0:T(8,128)(2,1)S(1)} %get-tuple-element.144), channel_id=1, source_target_pairs={{0,1},{1,2},{2,3},{3,0},{4,5},{5,6},{6,7},{7,4},{8,9},{9,10},{10,1... | collective-permute-start | bytes 749576 | tf_op jit(solution)/shard_map/ppermute | solution.py:66
  243.8 3.5 %collective-permute-start.40 = (bf16[16,7808]{1,0:T(8,128)(2,1)S(1)}, bf16[16,7808]{1,0:T(8,128)(2,1)S(1)}, u32[]{:S(2)}, u32[]{:S(2)}) collective-permute-start(bf16[16,7808]{1,0:T(8,128)(2,1)S(1)} %get-tuple-element.145), channel_id=1, source_target_pairs={{0,2},{1,3},{2,0},{3,1},{4,6},{5,7},{6,4},{7,5},{8,10},{9,11},{10,... | collective-permute-start | bytes 749576 | tf_op jit(solution)/shard_map/ppermute | solution.py:66
  248.3 3.9 %collective-permute-done.39.o1 = bf16[16,7808]{1,0:T(8,128)(2,1)S(1)} collective-permute-done((bf16[16,7808]{1,0:T(8,128)(2,1)S(1)}, bf16[16,7808]{1,0:T(8,128)(2,1)S(1)}, u32[]{:S(2)}, u32[]{:S(2)}) %collective-permute-start.39) | collective-permute-done | bytes 249888 | tf_op jit(solution)/shard_map/ppermute | solution.py:66
  252.2 3.0 %collective-permute-done.40.o2 = bf16[16,7808]{1,0:T(8,128)(2,1)S(1)} collective-permute-done((bf16[16,7808]{1,0:T(8,128)(2,1)S(1)}, bf16[16,7808]{1,0:T(8,128)(2,1)S(1)}, u32[]{:S(2)}, u32[]{:S(2)}) %collective-permute-start.40) | collective-permute-done | bytes 249888 | tf_op jit(solution)/shard_map/ppermute | solution.py:66
  (174 shorter events, 79.9 us)
Async XLA Ops:
  5.7 16.8 %collective-permute-start = (bf16[256,1024]{1,0:T(8,128)(2,1)S(1)}, bf16[256,1024]{1,0:T(8,128)(2,1)S(1)}, u32[]{:S(2)}, u32[]{:S(2)}) collective-permute-start(bf16[256,1024]{1,0:T(8,128)(2,1)S(1)} %pad_maximum_fusion.1), channel_id=1, source_target_pairs={{0,32},{1,33},{2,34},{3,35},{4,36},{5,37},{6,38},{7,39},{8,40},{9,... | collective-permute-start | bytes 1572872 | tf_op jit(solution)/shard_map/ppermute | solution.py:66
  10.5 12.0 %collective-permute-start.4 = (bf16[16,7808]{1,0:T(8,128)(2,1)S(1)}, bf16[16,7808]{1,0:T(8,128)(2,1)S(1)}, u32[]{:S(2)}, u32[]{:S(2)}) collective-permute-start(bf16[16,7808]{1,0:T(8,128)(2,1)S(1)} %shard_map.264.p0), channel_id=1, source_target_pairs={{0,3},{1,0},{2,1},{3,2},{4,7},{5,4},{6,5},{7,6},{8,11},{9,8},{10,9... | collective-permute-start | bytes 749576 | tf_op jit(solution)/shard_map/ppermute | solution.py:66
  24.3 12.0 %collective-permute-start.6 = (bf16[2,32,3712]{2,1,0:T(8,128)(2,1)}, bf16[2,32,3712]{2,1,0:T(8,128)(2,1)S(1)}, u32[]{:S(2)}, u32[]{:S(2)}) collective-permute-start(bf16[2,32,3712]{2,1,0:T(8,128)(2,1)} %get-tuple-element.88.refs_0_), channel_id=1, source_target_pairs={{0,8},{1,9},{2,10},{3,11},{4,12},{5,13},{6,14},{7,15},{8,16},{9,17... | collective-permute-start | bytes 1425416 | tf_op jit(solution)/shard_map/ppermute | solution.py:66
  26.3 12.4 %collective-permute-start.8 = (bf16[2,32,3712]{2,1,0:T(8,128)(2,1)}, bf16[2,32,3712]{2,1,0:T(8,128)(2,1)S(1)}, u32[]{:S(2)}, u32[]{:S(2)}) collective-permute-start(bf16[2,32,3712]{2,1,0:T(8,128)(2,1)} %get-tuple-element.89.refs_3_), channel_id=1, source_target_pairs={{0,4},{1,5},{2,6},{3,7},{4,64},{5,65},{6,66},{7,67},{8,12},{9,13},... | collective-permute-start | bytes 1425416 | tf_op jit(solution)/shard_map/ppermute | solution.py:66
  27.8 13.1 %collective-permute-start.10 = (bf16[2,32,3712]{2,1,0:T(8,128)(2,1)}, bf16[2,32,3712]{2,1,0:T(8,128)(2,1)S(1)}, u32[]{:S(2)}, u32[]{:S(2)}) collective-permute-start(bf16[2,32,3712]{2,1,0:T(8,128)(2,1)} %get-tuple-element.88.refs_0_), channel_id=1, source_target_pairs={{0,24},{1,25},{2,26},{3,27},{4,28},{5,29},{6,30},{7,31},{8,0},{9,1... | collective-permute-start | bytes 1425416 | tf_op jit(solution)/shard_map/ppermute | solution.py:66
  30.0 11.0 %collective-permute-start.11 = (bf16[2,32,3712]{2,1,0:T(8,128)(2,1)}, bf16[2,32,3712]{2,1,0:T(8,128)(2,1)}, u32[]{:S(2)}, u32[]{:S(2)}) collective-permute-start(bf16[2,32,3712]{2,1,0:T(8,128)(2,1)} %get-tuple-element.89.refs_3_), channel_id=1, source_target_pairs={{0,68},{1,69},{2,70},{3,71},{4,0},{5,1},{6,2},{7,3},{8,76},{9,77},... | collective-permute-start | bytes 1425416 | tf_op jit(solution)/shard_map/ppermute | solution.py:66
  36.4 11.5 %collective-permute-start.7 = (bf16[2,32,3712]{2,1,0:T(8,128)(2,1)S(1)}, bf16[2,32,3712]{2,1,0:T(8,128)(2,1)S(1)}, u32[]{:S(2)}, u32[]{:S(2)}) collective-permute-start(bf16[2,32,3712]{2,1,0:T(8,128)(2,1)S(1)} %collective-permute-done.6.refs_1_), channel_id=1, source_target_pairs={{0,8},{1,9},{2,10},{3,11},{4,12},{5,13},{6,14},{7,15},{8,16},{9,17... | collective-permute-start | bytes 1425416 | tf_op jit(solution)/shard_map/ppermute | solution.py:66
  51.0 19.5 %collective-permute-start.13 = (bf16[2,4,32,1408]{3,2,1,0:T(8,128)(2,1)}, bf16[2,4,32,1408]{3,2,1,0:T(8,128)(2,1)}, u32[]{:S(2)}, u32[]{:S(2)}) collective-permute-start(bf16[2,4,32,1408]{3,2,1,0:T(8,128)(2,1)} %get-tuple-element.94.p0.wp0), channel_id=1, source_target_pairs={{0,68},{1,69},{2,70},{3,71},{4,0},{5,1},{6,2},{7,3},{8,76},{9,77},... | collective-permute-start | bytes 2162696 | tf_op jit(solution)/shard_map/ppermute | solution.py:66
  53.2 19.7 %collective-permute-start.12 = (bf16[2,4,32,1408]{3,2,1,0:T(8,128)(2,1)}, bf16[2,4,32,1408]{3,2,1,0:T(8,128)(2,1)}, u32[]{:S(2)}, u32[]{:S(2)}) collective-permute-start(bf16[2,4,32,1408]{3,2,1,0:T(8,128)(2,1)} %get-tuple-element.94.p0.wp0), channel_id=1, source_target_pairs={{0,4},{1,5},{2,6},{3,7},{4,64},{5,65},{6,66},{7,67},{8,12},{9,13},... | collective-permute-start | bytes 2162696 | tf_op jit(solution)/shard_map/ppermute | solution.py:66
  53.2 20.4 %collective-permute-start.15 = (bf16[2,2,2,32,1408]{4,3,2,1,0:T(8,128)(2,1)}, bf16[2,2,2,32,1408]{4,3,2,1,0:T(8,128)(2,1)}, u32[]{:S(2)}, u32[]{:S(2)}) collective-permute-start(bf16[2,2,2,32,1408]{4,3,2,1,0:T(8,128)(2,1)} %get-tuple-element.95.q0.wq0), channel_id=1, source_target_pairs={{0,8},{1,9},{2,10},{3,11},{4,12},{5,13},{6,14},{7,15},{8,16},{9,17... | collective-permute-start | bytes 2162696 | tf_op jit(solution)/shard_map/ppermute | solution.py:66
  56.9 36.1 %collective-permute-start.19 = (bf16[2,4,32,2304]{3,2,1,0:T(8,128)(2,1)}, bf16[2,4,32,2304]{3,2,1,0:T(8,128)(2,1)S(1)}, u32[]{:S(2)}, u32[]{:S(2)}) collective-permute-start(bf16[2,4,32,2304]{3,2,1,0:T(8,128)(2,1)} %get-tuple-element.100.p0), channel_id=1, source_target_pairs={{0,4},{1,5},{2,6},{3,7},{4,64},{5,65},{6,66},{7,67},{8,12},{9,13},... | collective-permute-start | bytes 3538952 | tf_op jit(solution)/shard_map/ppermute | solution.py:66
  57.0 38.4 %collective-permute-start.22 = (bf16[2,2,2,32,2304]{4,3,2,1,0:T(8,128)(2,1)}, bf16[2,2,2,32,2304]{4,3,2,1,0:T(8,128)(2,1)}, u32[]{:S(2)}, u32[]{:S(2)}) collective-permute-start(bf16[2,2,2,32,2304]{4,3,2,1,0:T(8,128)(2,1)} %get-tuple-element.101.q0), channel_id=1, source_target_pairs={{0,8},{1,9},{2,10},{3,11},{4,12},{5,13},{6,14},{7,15},{8,16},{9,17... | collective-permute-start | bytes 3538952 | tf_op jit(solution)/shard_map/ppermute | solution.py:66
  70.4 21.0 %collective-permute-start.16 = (bf16[2,2,2,32,1408]{4,3,2,1,0:T(8,128)(2,1)}, bf16[2,2,2,32,1408]{4,3,2,1,0:T(8,128)(2,1)S(1)}, u32[]{:S(2)}, u32[]{:S(2)}) collective-permute-start(bf16[2,2,2,32,1408]{4,3,2,1,0:T(8,128)(2,1)} %get-tuple-element.95.q0.wq0), channel_id=1, source_target_pairs={{0,24},{1,25},{2,26},{3,27},{4,28},{5,29},{6,30},{7,31},{8,0},{9,1... | collective-permute-start | bytes 2162696 | tf_op jit(solution)/shard_map/ppermute | solution.py:66
  72.9 22.5 %collective-permute-start.14 = (bf16[2,4,32,1408]{3,2,1,0:T(8,128)(2,1)}, bf16[2,4,32,1408]{3,2,1,0:T(8,128)(2,1)S(1)}, u32[]{:S(2)}, u32[]{:S(2)}) collective-permute-start(bf16[2,4,32,1408]{3,2,1,0:T(8,128)(2,1)} %collective-permute-done.12.p1.wp1), channel_id=1, source_target_pairs={{0,4},{1,5},{2,6},{3,7},{4,64},{5,65},{6,66},{7,67},{8,12},{9,13},... | collective-permute-start | bytes 2162696 | tf_op jit(solution)/shard_map/ppermute | solution.py:66
  73.6 27.1 %collective-permute-start.17 = (bf16[2,2,2,32,1408]{4,3,2,1,0:T(8,128)(2,1)}, bf16[2,2,2,32,1408]{4,3,2,1,0:T(8,128)(2,1)S(1)}, u32[]{:S(2)}, u32[]{:S(2)}) collective-permute-start(bf16[2,2,2,32,1408]{4,3,2,1,0:T(8,128)(2,1)} %collective-permute-done.15.q1.wq1), channel_id=1, source_target_pairs={{0,8},{1,9},{2,10},{3,11},{4,12},{5,13},{6,14},{7,15},{8,16},{9,17... | collective-permute-start | bytes 2162696 | tf_op jit(solution)/shard_map/ppermute | solution.py:66
  91.5 24.2 %collective-permute-start.20 = (bf16[2,4,32,2304]{3,2,1,0:T(8,128)(2,1)S(1)}, bf16[2,4,32,2304]{3,2,1,0:T(8,128)(2,1)S(1)}, u32[]{:S(2)}, u32[]{:S(2)}) collective-permute-start(bf16[2,4,32,2304]{3,2,1,0:T(8,128)(2,1)S(1)} %copy-done), channel_id=1, source_target_pairs={{0,68},{1,69},{2,70},{3,71},{4,0},{5,1},{6,2},{7,3},{8,76},{9,77},... | collective-permute-start | bytes 3538952 | tf_op jit(solution)/shard_map/ppermute | solution.py:66
  93.0 25.6 %collective-permute-start.23 = (bf16[2,2,2,32,2304]{4,3,2,1,0:T(8,128)(2,1)}, bf16[2,2,2,32,2304]{4,3,2,1,0:T(8,128)(2,1)S(1)}, u32[]{:S(2)}, u32[]{:S(2)}) collective-permute-start(bf16[2,2,2,32,2304]{4,3,2,1,0:T(8,128)(2,1)} %get-tuple-element.101.q0), channel_id=1, source_target_pairs={{0,24},{1,25},{2,26},{3,27},{4,28},{5,29},{6,30},{7,31},{8,0},{9,1... | collective-permute-start | bytes 3538952 | tf_op jit(solution)/shard_map/ppermute | solution.py:66
  95.3 23.2 %collective-permute-start.21 = (bf16[2,4,32,2304]{3,2,1,0:T(8,128)(2,1)S(1)}, bf16[2,4,32,2304]{3,2,1,0:T(8,128)(2,1)S(1)}, u32[]{:S(2)}, u32[]{:S(2)}) collective-permute-start(bf16[2,4,32,2304]{3,2,1,0:T(8,128)(2,1)S(1)} %collective-permute-done.19.p1), channel_id=1, source_target_pairs={{0,4},{1,5},{2,6},{3,7},{4,64},{5,65},{6,66},{7,67},{8,12},{9,13},... | collective-permute-start | bytes 3538952 | tf_op jit(solution)/shard_map/ppermute | solution.py:66
  95.5 23.9 %collective-permute-start.24 = (bf16[2,2,2,32,2304]{4,3,2,1,0:T(8,128)(2,1)}, bf16[2,2,2,32,2304]{4,3,2,1,0:T(8,128)(2,1)S(1)}, u32[]{:S(2)}, u32[]{:S(2)}) collective-permute-start(bf16[2,2,2,32,2304]{4,3,2,1,0:T(8,128)(2,1)} %collective-permute-done.22.q1), channel_id=1, source_target_pairs={{0,8},{1,9},{2,10},{3,11},{4,12},{5,13},{6,14},{7,15},{8,16},{9,17... | collective-permute-start | bytes 3538952 | tf_op jit(solution)/shard_map/ppermute | solution.py:66
  134.3 29.1 %collective-permute-start.28 = (bf16[2,4,64,2304]{3,2,1,0:T(8,128)(2,1)}, bf16[2,4,64,2304]{3,2,1,0:T(8,128)(2,1)S(1)}, u32[]{:S(2)}, u32[]{:S(2)}) collective-permute-start(bf16[2,4,64,2304]{3,2,1,0:T(8,128)(2,1)} %get-tuple-element.124), channel_id=1, source_target_pairs={{0,4},{1,5},{2,6},{3,7},{4,0},{5,1},{6,2},{7,3},{8,12},{9,13},{10,... | collective-permute-start | bytes 7077896 | tf_op jit(solution)/shard_map/ppermute | solution.py:66
  135.4 29.1 %collective-permute-start.30 = (bf16[2,4,64,2304]{3,2,1,0:T(8,128)(2,1)}, bf16[2,4,64,2304]{3,2,1,0:T(8,128)(2,1)S(1)}, u32[]{:S(2)}, u32[]{:S(2)}) collective-permute-start(bf16[2,4,64,2304]{3,2,1,0:T(8,128)(2,1)} %get-tuple-element.128), channel_id=1, source_target_pairs={{0,8},{1,9},{2,10},{3,11},{4,12},{5,13},{6,14},{7,15},{8,0},{9,1},... | collective-permute-start | bytes 7077896 | tf_op jit(solution)/shard_map/ppermute | solution.py:66
  153.0 29.8 %collective-permute-start.27 = (bf16[2,4,64,1408]{3,2,1,0:T(8,128)(2,1)}, bf16[2,4,64,1408]{3,2,1,0:T(8,128)(2,1)S(1)}, u32[]{:S(2)}, u32[]{:S(2)}) collective-permute-start(bf16[2,4,64,1408]{3,2,1,0:T(8,128)(2,1)} %get-tuple-element.120), channel_id=1, source_target_pairs={{0,4},{1,5},{2,6},{3,7},{4,0},{5,1},{6,2},{7,3},{8,12},{9,13},{10,... | collective-permute-start | bytes 4325384 | tf_op jit(solution)/shard_map/ppermute | solution.py:66
  154.8 30.6 %collective-permute-start.29 = (bf16[2,4,64,1408]{3,2,1,0:T(8,128)(2,1)}, bf16[2,4,64,1408]{3,2,1,0:T(8,128)(2,1)S(1)}, u32[]{:S(2)}, u32[]{:S(2)}) collective-permute-start(bf16[2,4,64,1408]{3,2,1,0:T(8,128)(2,1)} %get-tuple-element.126), channel_id=1, source_target_pairs={{0,8},{1,9},{2,10},{3,11},{4,12},{5,13},{6,14},{7,15},{8,0},{9,1},... | collective-permute-start | bytes 4325384 | tf_op jit(solution)/shard_map/ppermute | solution.py:66
  169.6 29.1 %collective-permute-start.32 = (bf16[4,64,2304]{2,1,0:T(8,128)(2,1)}, bf16[4,64,2304]{2,1,0:T(8,128)(2,1)S(1)}, u32[]{:S(2)}, u32[]{:S(2)}) collective-permute-start(bf16[4,64,2304]{2,1,0:T(8,128)(2,1)} %get-tuple-element.132), channel_id=1, source_target_pairs={{0,68},{1,69},{2,70},{3,71},{4,64},{5,65},{6,66},{7,67},{8,76},{9,... | collective-permute-start | bytes 3538952 | tf_op jit(solution)/shard_map/ppermute | solution.py:66
  172.5 26.1 %collective-permute-start.34 = (bf16[4,64,2304]{2,1,0:T(8,128)(2,1)}, bf16[4,64,2304]{2,1,0:T(8,128)(2,1)}, u32[]{:S(2)}, u32[]{:S(2)}) collective-permute-start(bf16[4,64,2304]{2,1,0:T(8,128)(2,1)} %get-tuple-element.136), channel_id=1, source_target_pairs={{0,24},{1,25},{2,26},{3,27},{4,28},{5,29},{6,30},{7,31},{8,16},{9,... | collective-permute-start | bytes 3538952 | tf_op jit(solution)/shard_map/ppermute | solution.py:66
  189.5 12.9 %collective-permute-start.31 = (bf16[4,64,1408]{2,1,0:T(8,128)(2,1)}, bf16[4,64,1408]{2,1,0:T(8,128)(2,1)S(1)}, u32[]{:S(2)}, u32[]{:S(2)}) collective-permute-start(bf16[4,64,1408]{2,1,0:T(8,128)(2,1)} %get-tuple-element.130), channel_id=1, source_target_pairs={{0,68},{1,69},{2,70},{3,71},{4,64},{5,65},{6,66},{7,67},{8,76},{9,... | collective-permute-start | bytes 2162696 | tf_op jit(solution)/shard_map/ppermute | solution.py:66
  192.8 12.8 %collective-permute-start.33 = (bf16[4,64,1408]{2,1,0:T(8,128)(2,1)}, bf16[4,64,1408]{2,1,0:T(8,128)(2,1)}, u32[]{:S(2)}, u32[]{:S(2)}) collective-permute-start(bf16[4,64,1408]{2,1,0:T(8,128)(2,1)} %get-tuple-element.134), channel_id=1, source_target_pairs={{0,24},{1,25},{2,26},{3,27},{4,28},{5,29},{6,30},{7,31},{8,16},{9,... | collective-permute-start | bytes 2162696 | tf_op jit(solution)/shard_map/ppermute | solution.py:66
  209.2 14.0 %collective-permute-start.35 = (bf16[2,64,3712]{2,1,0:T(8,128)(2,1)}, bf16[2,64,3712]{2,1,0:T(8,128)(2,1)S(1)}, u32[]{:S(2)}, u32[]{:S(2)}) collective-permute-start(bf16[2,64,3712]{2,1,0:T(8,128)(2,1)} %get-tuple-element.138), channel_id=1, source_target_pairs={{0,8},{1,9},{2,10},{3,11},{4,12},{5,13},{6,14},{7,15},{8,0},{9,1},... | collective-permute-start | bytes 2850824 | tf_op jit(solution)/shard_map/ppermute | solution.py:66
  209.3 14.0 %collective-permute-start.36 = (bf16[2,64,3712]{2,1,0:T(8,128)(2,1)}, bf16[2,64,3712]{2,1,0:T(8,128)(2,1)S(1)}, u32[]{:S(2)}, u32[]{:S(2)}) collective-permute-start(bf16[2,64,3712]{2,1,0:T(8,128)(2,1)} %get-tuple-element.140), channel_id=1, source_target_pairs={{0,4},{1,5},{2,6},{3,7},{4,0},{5,1},{6,2},{7,3},{8,12},{9,13},{10,... | collective-permute-start | bytes 2850824 | tf_op jit(solution)/shard_map/ppermute | solution.py:66
  212.1 18.0 %collective-permute-start.26 = (f32[128,1024]{1,0:T(8,128)}, f32[128,1024]{1,0:T(8,128)S(1)}, u32[]{:S(2)}, u32[]{:S(2)}) collective-permute-start(f32[128,1024]{1,0:T(8,128)} %get-tuple-element.117), channel_id=1, source_target_pairs={{0,32},{1,33},{2,34},{3,35},{4,36},{5,37},{6,38},{7,39},{8,40},{9,... | collective-permute-start | bytes 1572872 | tf_op jit(solution)/shard_map/ppermute | solution.py:66
  240.9 11.3 %collective-permute-start.39 = (bf16[16,7808]{1,0:T(8,128)(2,1)S(1)}, bf16[16,7808]{1,0:T(8,128)(2,1)S(1)}, u32[]{:S(2)}, u32[]{:S(2)}) collective-permute-start(bf16[16,7808]{1,0:T(8,128)(2,1)S(1)} %get-tuple-element.144), channel_id=1, source_target_pairs={{0,1},{1,2},{2,3},{3,0},{4,5},{5,6},{6,7},{7,4},{8,9},{9,10},{10,1... | collective-permute-start | bytes 749576 | tf_op jit(solution)/shard_map/ppermute | solution.py:66
  243.8 11.4 %collective-permute-start.40 = (bf16[16,7808]{1,0:T(8,128)(2,1)S(1)}, bf16[16,7808]{1,0:T(8,128)(2,1)S(1)}, u32[]{:S(2)}, u32[]{:S(2)}) collective-permute-start(bf16[16,7808]{1,0:T(8,128)(2,1)S(1)} %get-tuple-element.145), channel_id=1, source_target_pairs={{0,2},{1,3},{2,0},{3,1},{4,6},{5,7},{6,4},{7,5},{8,10},{9,11},{10,... | collective-permute-start | bytes 749576 | tf_op jit(solution)/shard_map/ppermute | solution.py:66
  (34 other events, 255.0 us)
